TPU v7x, 512 devices: a whole 4x4x16 slice. The times are simulated.
512 devices in a mesh: dx: 16 (over y, x), dy: 32 (over z, core).
Axes of the slice: x: 4, y: 4, z: 16, core: 2. Of those that a mesh axis runs over, the one named last changes fastest.
Arguments:
- audio: bfloat16 [32, 128, 2570], P('dy', 'dx'), may hold values from -6 to 6
- counts: int32 [32, 16], P('dy', 'dx'), may hold values from 1 to 8, 64 in all within a row
- cotangent: bfloat16 [32, 64, 256, 512], P('dy', 'dx'), may hold values from -6 to 6
- conv_first: bfloat16 [10, 512], replicated, may hold values from -2 to 2
- norm_gain: float32 [512], replicated, may hold values from 0.1 to 1.9
- norm_bias: float32 [512], replicated, may hold values from -3 to 3
- conv_second: bfloat16 [1536, 512], replicated, may hold values from -0.15625 to 0.15625
Outputs:
- grad_conv_first: float32 [10, 512], replicated
- grad_norm: float32 [2, 512], replicated
- grad_conv_second: float32 [1536, 512], P('dy')
Inputs may be any that keep to these rules, and one draw needn't show every extreme that they name: In each group along dy the counts sum to 64, and some device of each group holds exactly 8 live crops.
All inputs are finite; a program needn't handle non-finite values.
Results may differ from a plain program's by a relative error of at most 0.0051.
Values may be sent and summed in bfloat16 or wider, within the bound.
A program may use at most 128 MiB of HBM per device.

v0:
```python
import math

import jax
import jax.numpy as jnp
from jax import lax
from jax.sharding import PartitionSpec as P


def gelu_cdf(value):
    return 0.5 * (1.0 + lax.erf(value * 0.7071067811865476))


def gelu_slope(value):
    return gelu_cdf(value) + value * jnp.exp(-0.5 * value * value) * 0.3989422804014327


def forward_backward(
    crop_waves, cot_rows, conv_first, norm_gain, norm_bias, conv_second, loss_scale
):
    batch_size = crop_waves.shape[0]
    frames = cot_rows.shape[1]
    first_len = 2 * frames + 1
    channels = conv_second.shape[1]
    early_taps = crop_waves[:, : 5 * first_len].reshape(batch_size, first_len, 5)
    late_taps = crop_waves[:, 5 : 5 * first_len + 5].reshape(batch_size, first_len, 5)
    patches = jnp.concatenate([early_taps, late_taps], axis=2).reshape(batch_size * first_len, 10)
    pre_norm = jnp.dot(patches, conv_first, preferred_element_type=jnp.float32).reshape(
        batch_size, first_len, channels
    )
    centre = pre_norm - jnp.mean(pre_norm, axis=1, keepdims=True)
    inv_std = lax.rsqrt(jnp.mean(centre * centre, axis=1, keepdims=True) + 1e-05)
    normed = centre * inv_std
    shifted = normed * norm_gain + norm_bias
    hidden = (shifted * gelu_cdf(shifted)).astype(jnp.bfloat16)
    two_taps = hidden[:, : 2 * frames].reshape(batch_size, frames, 2 * channels)
    third_tap = hidden[:, 2::2]
    second_rows = jnp.concatenate([two_taps, third_tap], axis=2).reshape(
        batch_size * frames, 3 * channels
    )
    pre_act = jnp.dot(second_rows, conv_second, preferred_element_type=jnp.float32)
    grad_rows = (
        loss_scale
        * cot_rows.reshape(batch_size * frames, channels).astype(jnp.float32)
        * gelu_slope(pre_act)
    ).astype(jnp.bfloat16)
    grad_cols = jnp.dot(grad_rows, conv_second.T, preferred_element_type=jnp.float32).reshape(
        batch_size, frames, 3 * channels
    )
    first_taps = grad_cols[:, :, : 2 * channels].reshape(batch_size, 2 * frames, channels)
    late_tap = jnp.stack(
        [grad_cols[:, :, 2 * channels :], jnp.zeros((batch_size, frames, channels), jnp.float32)],
        axis=2,
    ).reshape(batch_size, 2 * frames, channels)
    grad_hidden = jnp.concatenate(
        [first_taps, jnp.zeros((batch_size, 1, channels), jnp.float32)], axis=1
    )
    grad_hidden = grad_hidden + jnp.concatenate(
        [jnp.zeros((batch_size, 2, channels), jnp.float32), late_tap[:, : 2 * frames - 1]], axis=1
    )
    grad_shift = grad_hidden * gelu_slope(shifted)
    gain_grad = jnp.sum(grad_shift * normed, axis=(0, 1))
    shift_grad = jnp.sum(grad_shift, axis=(0, 1))
    grad_scaled = grad_shift * norm_gain
    grad_pre = inv_std * (
        grad_scaled
        - jnp.mean(grad_scaled, axis=1, keepdims=True)
        - normed * jnp.mean(grad_scaled * normed, axis=1, keepdims=True)
    )
    grad_pre = grad_pre.astype(jnp.bfloat16).reshape(batch_size * first_len, channels)
    grad_first = jnp.dot(patches.T, grad_pre, preferred_element_type=jnp.float32)
    return (second_rows, grad_rows, grad_first, jnp.stack([gain_grad, shift_grad]))


def on_device(audio, counts, cotangent, conv_first, norm_gain, norm_bias, conv_second):
    groups = lax.axis_size("dx")
    position = lax.axis_index("dx")
    slot_count = audio.shape[1]
    receive = cotangent.shape[1]
    frames = cotangent.shape[2]
    all_counts = lax.all_gather(counts, "dx", axis=1, tiled=True)[0]
    starts = jnp.cumsum(all_counts, dtype=jnp.int32) - all_counts
    everything = lax.all_gather(audio, "dx", axis=1, tiled=True)[0]
    wanted = jnp.arange(receive, dtype=jnp.int32) * groups + position
    holder = (
        jnp.sum((starts[None, :] <= wanted[:, None]).astype(jnp.int32), axis=1, dtype=jnp.int32) - 1
    )
    offset = wanted - starts[holder]
    crop_waves = jnp.take(everything, holder * slot_count + offset, axis=0)
    loss_scale = 1.0 / math.sqrt(groups * lax.axis_size("dy") * receive * frames)
    second_rows, grad_rows, grad_first, grad_gains = forward_backward(
        crop_waves, cotangent[0], conv_first, norm_gain, norm_bias, conv_second, loss_scale
    )
    row_share = conv_second.shape[0] // lax.axis_size("dy")
    grad_second = jnp.dot(second_rows.T, grad_rows, preferred_element_type=jnp.float32)
    summed_first, summed_gains, whole_second = lax.psum(
        (grad_first, grad_gains, grad_second), ("dx", "dy")
    )
    summed_second = lax.dynamic_slice_in_dim(
        whole_second, lax.axis_index("dy") * row_share, row_share, 0
    )
    return (summed_first, summed_gains, summed_second)


def solution(mesh):
    in_specs = (P("dy", "dx", None), P("dy", "dx"), P("dy", "dx", None, None), P(), P(), P(), P())
    out_specs = (P(), P(), P("dy", None))
    return jax.shard_map(
        on_device, mesh=mesh, in_specs=in_specs, out_specs=out_specs, check_vma=False
    )
```

profile of v0, /device:TPU:1, one launch (start us, length us, event | category | flops | bytes accessed | tf_op | source)
XLA Modules:
  0.0 582.6 jit_solution(14442549444901075429)
XLA Ops:
  7.2 0.0 copy-start
  7.2 0.0 all-reduce.7.cloned.1.call-start
  8.0 1.3 dynamic-slice
  9.3 0.7 bitcast_dynamic-update-slice_fusion
  9.9 13.9 %all-reduce.3 = s32[16]{0:T(128)S(1)} all-reduce(s32[16]{0:T(128)S(1)} %bitcast_dynamic-update-slice_fusion), channel_id=1, replica_groups=mesh['dx'=16,'dy'=32] {'dx'}, use_global_device_ids=true, to_apply=%add.3 | all-reduce | flops 16 | bytes 128 | tf_op jit(solution)/shard_map/squeeze | solution.py:80
  23.9 0.1 copy.14
  24.0 0.1 reduce
  24.1 0.2 convert_reduce_fusion
  24.3 0.6 gather_fusion
  25.0 17.5 %all_gather.7 = bf16[1,128,2570]{2,1,0:T(8,128)(2,1)S(1)} all-gather(bf16[1,8,2570]{2,1,0:T(8,128)(2,1)} %param.7), channel_id=1, replica_groups=mesh['dx'=16,'dy'=32] {'dx'}, dimensions={1}, use_global_device_ids=true | all-gather | bytes 699040 | tf_op jit(solution)/shard_map/all_gather | solution.py:82
  42.6 0.6 gather_fusion.1
  43.1 0.1 broadcast_select_fusion
  43.2 0.1 fusion.26
  43.3 0.4 reshape.141
  43.7 0.3 copy.15
  44.0 0.4 reshape.142
  44.4 0.3 copy.16
  44.7 0.0 copy-start.5
  44.7 0.0 copy-start.6
  44.7 1.5 fusion.27
  46.2 0.0 copy-start.1
  46.2 0.6 multiply_reduce_fusion.2
  46.8 1.3 copy-done.1
  48.2 0.0 copy-done.5
  48.2 0.0 copy-done.6
  48.2 2.4 multiply_convert_fusion.1
  50.6 0.0 copy-start.3
  50.6 11.7 %slice.24 = bf16[4,256,512]{2,1,0:T(8,128)(2,1)} slice(bf16[4,513,512]{2,1,0:T(8,128)(2,1)} %multiply_convert_fusion.1), slice={[0:4:1], [2:513:2], [0:512:1]} | slice | bytes 2097152 | tf_op jit(solution)/shard_map/slice | solution.py:36
  62.2 3.1 slice.34
  65.3 0.0 copy-done.3
  65.3 1.6 convert_multiply_fusion
  66.9 4.1 concatenate.20
  71.0 0.0 copy-done
  71.0 0.0 copy-start.2
  71.0 0.0 copy-start.4
  71.0 5.1 fusion.11
  76.1 0.0 copy-done.2
  76.1 0.0 copy-done.4
  76.1 3.6 fusion.12
  79.7 0.0 all-reduce.7.cloned.1.call-update
  79.7 1.8 fusion.28
  81.5 1.5 slice.36
  83.0 2.4 slice.35
  85.4 4.9 reshape.144
  90.3 3.0 stack.15
  93.4 3.4 stack.16
  96.8 0.0 slice-start
  96.8 6.1 %reshape.145 = f32[4,512,512]{2,1,0:T(8,128)} reshape(f32[4,256,2,512]{3,2,1,0:T(2,128)} %stack.16) | data formatting | bytes 8388608 | tf_op jit(solution)/shard_map/reshape | solution.py:53
  102.8 0.0 slice-start.1
  102.8 7.4 %multiply_reduce_fusion = (f32[512]{0:T(512)S(1)}, f32[4,512]{1,0:T(4,128)S(1)}, f32[4,512]{1,0:T(4,128)S(1)}, f32[512]{0:T(512)S(1)}, f32[4,513,512]{2,1,0:T(8,128)S(1)}) fusion(f32[4,512]{1,0:T(4,128)S(1)} %add_rsqrt_fusion, f32[4,513,512]{2,1,0:T(8,128)} %copy-done.1, f32[4,512]{1,0:T(4,128)S(1)} %broadcast_multiply_fusion.2, f32[512]{0:T(512)S(1)} %copy-done.5, ...), kind=kLoop, calls=%fused_computation.8 | loop fusion | flops 22057984 | bytes 16826368 | tf_op jit(solution)/shard_map/reduce_sum | solution.py:61
  110.3 0.0 slice-done
  110.3 0.0 slice-done.1
  110.3 1.4 fusion.14
  111.7 116.9 %all-reduce.4 = (f32[10,512]{1,0:T(8,128)}, f32[2,512]{1,0:T(2,128)}) all-reduce(f32[10,512]{1,0:T(8,128)S(1)} %fusion.14, f32[2,512]{1,0:T(2,128)S(1)} %pad_maximum_fusion.8), channel_id=1, replica_groups=mesh['dx'=16,'dy'=32] {'dx','dy'}, use_global_device_ids=true, to_apply=%region_6.7 | all-reduce | flops 6144 | bytes 49152 | tf_op jit(solution)/shard_map/psum | solution.py:95
  228.6 345.7 %all-reduce.7.cloned.1.call-done = f32[1536,512]{1,0:T(8,128)} async-done(((f32[1536,512]{1,0:T(8,128)}), f32[1536,512]{1,0:T(8,128)}) %all-reduce.7.cloned.1.call-update) | async-done | bytes 3145744 | tf_op jit(solution)/shard_map/psum | solution.py:95
  574.2 1.5 constant_dynamic-slice_fusion
  (15 shorter events, 0.1 us)
Async XLA Ops:
  7.2 63.8 %copy-start = (bf16[1536,512]{1,0:T(8,128)(2,1)S(1)}, bf16[1536,512]{1,0:T(8,128)(2,1)}, u32[]{:S(2)}) copy-start(bf16[1536,512]{1,0:T(8,128)(2,1)} %param.13) | copy-start | bytes 4718596
  7.2 567.1 %all-reduce.7.cloned.1.call-start = ((), (), s32[]{:S(2)}) async-start(), calls=%async_computation | async-start | bytes 6291456 | tf_op jit(solution)/shard_map/psum | solution.py:95
  44.7 3.5 copy-start.5
  44.7 3.5 copy-start.6
  46.2 2.0 copy-start.1
  50.6 14.7 %copy-start.3 = (bf16[1,4,256,512]{3,2,1,0:T(8,128)(2,1)S(1)}, bf16[1,4,256,512]{3,2,1,0:T(8,128)(2,1)}, u32[]{:S(2)}) copy-start(bf16[1,4,256,512]{3,2,1,0:T(8,128)(2,1)} %param.9) | copy-start | bytes 3145732
  71.0 5.1 copy-start.2
  71.0 5.1 copy-start.4
  96.8 13.5 %slice-start = ((s8[4259840]{0:T(1024)(128)(4,1)}), s8[65536]{0:T(1024)(128)(4,1)S(1)}, s32[]{:S(2)}) async-start(s8[4259840]{0:T(1024)(128)(4,1)} %bitcast.48), calls=%async_computation.1 | async-start | bytes 131072
  102.8 7.5 %slice-start.1 = ((s8[4259840]{0:T(1024)(128)(4,1)}), s8[4194304]{0:T(1024)(128)(4,1)S(1)}, s32[]{:S(2)}) async-start(s8[4259840]{0:T(1024)(128)(4,1)} %bitcast.48), calls=%async_computation.2 | async-start | bytes 8388608
Sparse Core Ops, SparseCore 0:
  79.8 494.3 all-reduce.6
where the time goes:
time: 584 us; the launch traced here: 583 us
  waiting for transfers between devices  346 us (59%)
  blocking collectives  148 us (25%)
  local copies, waits for them, and re-layouts  47.7 us (8%)
  between operations  15 us (3%)
  matrix products  13.3 us (2%)
  other arithmetic  12.5 us (2%)
    psum x1, waiting for transfers between devices, on_device(): lax.psum((grad_first, grad_gains, grad_second), ('dx', 'dy'))  346 us
    psum x1, blocking collectives, on_device(): lax.psum((grad_first, grad_gains, grad_second), ('dx', 'dy'))  117 us
    all_gather x1, blocking collectives, on_device(): everything = lax.all_gather(audio, 'dx', axis=1, tiled=True)[0]  17.5 us
    squeeze x1, blocking collectives, on_device(): all_counts = lax.all_gather(counts, 'dx', axis=1, tiled=True)[0]  13.9 us
  transfers between devices with their start and end apart: 1, of which 1 were waited for; matrix products, arithmetic and copies ran while one was open for 5% of the time, Pallas kernels for 0%

commit v1 on v0

v1 whole, which is shorter than its diff:
```python
import functools
import math

import jax
import jax.numpy as jnp
from jax import lax
from jax.experimental import pallas as pl
from jax.experimental.pallas import tpu as pltpu
from jax.sharding import PartitionSpec as P

F32 = jnp.float32
BF16 = jnp.bfloat16
MESH = pl.DeviceIdType.MESH
SIDE = 4
TN = (((0,), (0,)), ((), ()))
NT = (((1,), (1,)), ((), ()))
NN = (((1,), (0,)), ((), ()))
LOG2E = 1.4426950408889634


def dot(a, b, dims=NN):
    return lax.dot_general(a, b, dims, preferred_element_type=F32)


def pieces(value):
    high = value.astype(BF16)
    rest = value - high.astype(F32)
    mid = rest.astype(BF16)
    low = (rest - mid.astype(F32)).astype(BF16)
    return high, mid, low


def gelu_parts(value):
    cdf = 0.5 * lax.erf(value * 0.7071067811865476) + 0.5
    slope = cdf + value * (jnp.exp2(value * value * (-0.5 * LOG2E)) * 0.3989422804014327)
    return cdf, slope


def rows_of(shape):
    return lax.broadcasted_iota(jnp.int32, shape, 0)


def cols_of(shape):
    return lax.broadcasted_iota(jnp.int32, shape, 1)


def kernel(
    planes, depth, scale,
    audio_hbm, counts_ref, cot_hbm, w1_hbm, gain_hbm, bias_hbm, w2_hbm,
    first_out, norm_out, second_out,
    audio, cot, w1, gain_ref, bias_ref, w2, load_sem,
    perm, zbuf, cnt_all, crop_send, crop_recv, xf, xp, weo, wpad, waug, gw, stat, colsum,
    hid, grows, slope_e, slope_o, slope_t, hshift, dshift,
    half_sum, pair_send, pair_recv,
    x_send, x_recv, y_send, y_recv, xa, ya, x2_send, x2_recv, y2_send, y2_recv,
    part, z_send, z_recv, full, gathered,
    acc_e, acc_o, acc_t, small, s_send, s_recv, u_val, u_recv, v_val, v_recv,
    cnt_ss, cnt_rs, crop_ss, crop_rs, pair_ss, pair_rs, plane_ss, plane_rs,
    z_ss, z_rs, d_ss, d_rs, s1_ss, s1_rs, s2_ss, s2_rs, s3_ss, s3_rs,
):
    me = lax.axis_index("dx")
    dy = lax.axis_index("dy")
    core = lax.rem(dy, 2)
    z = dy // 2
    px = lax.rem(me, SIDE)
    py = me // SIDE
    zhalf = depth // 2
    frames = cot_hbm.shape[2]
    channels = w2_hbm.shape[1]
    rows_all = w2_hbm.shape[0]
    half_rows = rows_all // 2
    rz = rows_all // depth
    rx = rz // SIDE
    hz = zhalf // 2
    hrows = half_rows // 2
    total_frames = 2 * frames + 1
    crops = cot_hbm.shape[1]

    def send(src, dst, ss, rs, where):
        return pltpu.make_async_remote_copy(
            src_ref=src, dst_ref=dst, send_sem=ss, recv_sem=rs,
            device_id=where, device_id_type=MESH,
        )

    loads = [
        pltpu.make_async_copy(src, dst, load_sem.at[i])
        for i, (src, dst) in enumerate(
            ((audio_hbm, audio), (w1_hbm, w1), (gain_hbm, gain_ref), (bias_hbm, bias_ref),
             (w2_hbm, w2), (cot_hbm, cot))
        )
    ]
    for load in loads:
        load.start()

    barrier = pltpu.get_barrier_semaphore()

    @pl.loop(0, planes)
    def _(p):
        @pl.when(p != me)
        def _():
            pl.semaphore_signal(barrier, inc=1, device_id=(p, dy), device_id_type=MESH)

        pl.semaphore_signal(barrier, inc=1, device_id=(p, 2 * z + 1 - core), device_id_type=MESH)

    @pl.loop(0, depth)
    def _(k):
        @pl.when(k != z)
        def _():
            pl.semaphore_signal(barrier, inc=1, device_id=(me, 2 * k + core), device_id_type=MESH)

    lane = cols_of((1, 640))
    sample = 10 * (lane % 64) + 2 * (lane // 128) + (lane % 128) // 64
    for i in range(5):
        block = rows_of((128, 640)) + 128 * i
        perm[pl.ds(128 * i, 128), :] = jnp.where(block == sample, 1.0, 0.0).astype(BF16)
    cnt_all[me] = jnp.full((1, 128), counts_ref[0, 0], jnp.int32)

    loads[0].wait()
    blocks = jnp.concatenate(
        [audio[0, :, 640 * i : 640 * i + 640].astype(F32) for i in range(4)], axis=0
    ).astype(BF16)
    sorted_blocks = dot(blocks, perm[...])
    eye = jnp.where(rows_of((10, 256)) == cols_of((10, 256)), 1.0, 0.0).astype(BF16)
    tails = dot(audio[0, :, 2560:2570], eye)
    low_lane = cols_of((8, 128)) < 64
    last_lane = cols_of((8, 256)) == 255
    for m in range(10):
        g = m // 2
        parts = []
        for half in range(2):
            a = sorted_blocks[16 * half : 16 * half + 8, 128 * g : 128 * g + 128]
            b = sorted_blocks[16 * half + 8 : 16 * half + 16, 128 * g : 128 * g + 128]
            if m % 2 == 0:
                parts.append(jnp.where(low_lane, a, pltpu.roll(b, 64, 1)))
            else:
                parts.append(jnp.where(low_lane, pltpu.roll(a, 64, 1), b))
        row = jnp.concatenate(parts, axis=1)
        zbuf[:, m, :] = row
        if m < 5:
            zbuf[:, 11 + m, :] = jnp.where(last_lane, tails[:, m : m + 1], pltpu.roll(row, 255, 1))
    zbuf[:, 10, :] = tails
    slot_rows = zbuf[...].reshape(128, 256).astype(BF16)

    waug[...] = jnp.zeros_like(waug)
    loads[1].wait()
    loads[2].wait()
    loads[3].wait()
    w1v = w1[...].astype(F32)
    weo[...] = jnp.zeros_like(weo)
    weo[0:10, 0:channels] = w1v
    weo[5:10, channels:] = w1v[0:5]
    weo[11:16, channels:] = w1v[5:10]
    wpad[...] = jnp.zeros_like(wpad)
    wpad[0:10, :] = w1v

    pl.semaphore_wait(barrier, 2 * planes - 1 + depth - 1)

    @pl.loop(1, planes)
    def _(k):
        to = lax.rem(me + k, planes)
        send(cnt_all.at[me], cnt_all.at[me], cnt_ss.at[k], cnt_rs.at[k], (to, dy)).start()

    @pl.loop(1, planes)
    def _(k):
        frm = lax.rem(me - k + planes, planes)
        send(cnt_all.at[me], cnt_all.at[frm], cnt_ss.at[k], cnt_rs.at[k], (frm, dy)).wait()

    count_rows = cnt_all[...].reshape(planes, 128)
    who = rows_of((planes, 128))
    start_me = jnp.sum(jnp.where(who < me, count_rows, 0), axis=0, keepdims=True)
    count_me = jnp.sum(jnp.where(who == me, count_rows, 0), axis=0, keepdims=True)
    shape = (16 * planes, 128)
    rr, cc = rows_of(shape), cols_of(shape)
    slot = cc // 16
    pick = (rr % 16 == cc % 16) & (slot < count_me) & ((start_me + slot) % planes == rr // 16)
    routed = dot(jnp.where(pick, 1.0, 0.0).astype(BF16), slot_rows).astype(BF16)
    crop_send[...] = routed.reshape(planes, 16, 256)

    @pl.loop(1, planes)
    def _(k):
        to = lax.rem(me + k, planes)
        send(crop_send.at[to], crop_recv.at[me], crop_ss.at[k], crop_rs.at[k], (to, dy)).start()

    crop_recv[me] = crop_send[me]
    wide = jnp.concatenate([count_rows, count_rows], axis=1)
    who2, col2 = rows_of((planes, 256)), cols_of((planes, 256)) // 16
    start_col = jnp.sum(jnp.where(who2 < col2, wide, 0), axis=0, keepdims=True)
    count_col = jnp.sum(jnp.where(who2 == col2, wide, 0), axis=0, keepdims=True)
    shape = (16 * crops, 256)
    rr, cc = rows_of(shape), cols_of(shape)
    order = (rr // 16) * planes + me
    pick = (rr % 16 == cc % 16) & (start_col <= order) & (order < start_col + count_col)
    pick = jnp.where(pick, 1.0, 0.0).astype(BF16)

    @pl.loop(1, planes)
    def _(k):
        frm = lax.rem(me - k + planes, planes)
        send(crop_send.at[frm], crop_recv.at[frm], crop_ss.at[k], crop_rs.at[k], (frm, dy)).wait()

    mine = dot(pick, crop_recv[...].reshape(16 * planes, 256))
    xf[...] = mine
    xp_all = jnp.where(rows_of((16 * crops, 256)) % 16 == 10, 1.0, mine)
    xp[...] = xp_all.astype(BF16)
    xt = jnp.concatenate([xp_all] * 3, axis=0).T.astype(BF16)

    tail_rows = jnp.concatenate(
        [xf[16 * r + 10 : 16 * r + 11, 0:128] for r in range(crops)]
        + [jnp.zeros((8 - crops, 128), F32)], axis=0)
    tail_pre = dot(tail_rows.astype(BF16), wpad[...].astype(BF16))
    gain = gain_ref[...].reshape(1, channels)
    bias = bias_ref[...].reshape(1, channels)
    we, wo = weo[:, 0:channels], weo[:, channels:]
    weo16 = weo[...].astype(BF16)
    row16 = rows_of((16, channels))
    for r in range(crops):
        x16 = xp[16 * r : 16 * r + 16, :]
        gram = dot(x16, x16, NT)
        g1, g2, g3 = pieces(gram)
        gwv = dot(g1, weo16) + dot(g2, weo16) + dot(g3, weo16)
        gw[r] = gwv
        colsum[r] = jnp.broadcast_to(gram[:, 10:11], (16, 128))
        pre_t = tail_pre[r : r + 1]
        gwe, gwo = gwv[:, 0:channels], gwv[:, channels:]
        mu = (gwe[10:11] + gwo[10:11] + pre_t) * (1.0 / total_frames)
        square = jnp.sum(we * gwe + wo * gwo, axis=0, keepdims=True) + pre_t * pre_t
        var = jnp.maximum(square * (1.0 / total_frames) - mu * mu, 0.0)
        inv = lax.rsqrt(var + 1e-5)
        mul = inv * gain
        add = bias - mu * mul
        stat[r, 0:1] = mu
        stat[r, 1:2] = inv
        stat[r, 2:3] = mul
        stat[r, 3:4] = pre_t
        stat[r, 4:5] = pre_t * mul + add
        for side, w in ((0, we), (1, wo)):
            scaled = jnp.where(row16 == 10, add, w * mul)
            for i, piece in enumerate(pieces(scaled)):
                waug[r, 64 * i + 16 * r : 64 * i + 16 * r + 16,
                     side * channels : (side + 1) * channels] = piece

    loads[4].wait()
    loads[5].wait()
    quarter = channels // 2
    xt_parts = [xt[128 * i : 128 * i + 128] for i in range(frames // 128)]

    @pl.loop(0, crops)
    def _(r):
        base = pl.multiple_of(r * frames, frames)
        tail = stat[r, 4:5]
        cdf, slope = gelu_parts(tail)
        hshift[frames : frames + 1, :] = tail * cdf
        slope_t[r] = slope
        for n in range(4):
            for i in range(frames // 128):
                value = dot(xt_parts[i], waug[r, :, n * quarter : (n + 1) * quarter])
                cdf, slope = gelu_parts(value)
                value = value * cdf
                lo = (n % 2) * quarter
                if n < 2:
                    slope_e[r, 128 * i : 128 * i + 128, lo : lo + quarter] = slope
                    hshift[128 * i : 128 * i + 128, lo : lo + quarter] = value
                    hid[0, pl.ds(base + 128 * i, 128), lo : lo + quarter] = value.astype(BF16)
                else:
                    slope_o[r, 128 * i : 128 * i + 128, lo : lo + quarter] = slope
                    at = 512 if n == 2 else 0
                    hid[n - 2, pl.ds(base + 128 * i, 128), at : at + quarter] = value.astype(BF16)
        hid[1, pl.ds(base, frames), quarter:] = hshift[1 : frames + 1, :].astype(BF16)
        for n in range(2):
            cols = slice(n * quarter, (n + 1) * quarter)
            pre = dot(hid[0, pl.ds(base, frames), :], w2[0:half_rows, cols])
            pre = pre + dot(hid[1, pl.ds(base, frames), :], w2[half_rows:, cols])
            slope = gelu_parts(pre)[1]
            grad = (scale * cot[0, r, :, cols].astype(F32)) * slope
            grows[pl.ds(base, frames), cols] = grad.astype(BF16)

    pair = (me, 2 * z + 1 - core)
    for h in range(2):
        theirs = dot(hid[1 - core, :, h * hrows : (h + 1) * hrows], grows[...], TN)
        pair_send[h] = theirs.astype(BF16)
        send(pair_send.at[h], pair_recv.at[h], pair_ss.at[h], pair_rs.at[h], pair).start()
    for h in range(2):
        half_sum[h] = dot(hid[core, :, h * hrows : (h + 1) * hrows], grows[...], TN)

    acc_e[...] = jnp.zeros_like(acc_e)
    acc_o[...] = jnp.zeros_like(acc_o)
    acc_t[...] = jnp.zeros_like(acc_t)
    small[...] = jnp.zeros_like(small)
    dshift[0:8, :] = jnp.zeros((8, channels), F32)

    def backward(r):
        base = pl.multiple_of(r * frames, frames)
        grad = grows[pl.ds(base, frames), :]
        x16 = xp[pl.ds(pl.multiple_of(16 * r, 16), 16), :]
        shift_o = dot(grad, w2[channels : 2 * channels, :], NT) * slope_o[r]
        p_o = dot(x16, shift_o.astype(BF16))
        dshift[8 : 8 + frames, :] = dot(grad, w2[2 * channels :, :], NT)
        shift_e = dot(grad, w2[0:channels, :], NT) + dshift[7 : 7 + frames, :]
        p_e = dot(x16, (shift_e * slope_e[r]).astype(BF16))
        shift_t = dshift[7 + frames : 8 + frames, :] * slope_t[r]
        mu, inv, mul, pre_t = stat[r, 0:1], stat[r, 1:2], stat[r, 2:3], stat[r, 3:4]
        total = p_e[10:11] + p_o[10:11] + shift_t
        with_pre = jnp.sum(weo[:, 0:channels] * p_e + weo[:, channels:] * p_o, axis=0, keepdims=True)
        with_norm = inv * (with_pre + pre_t * shift_t - mu * total)
        small[10:11, :] = small[10:11, :] + with_norm
        small[11:12, :] = small[11:12, :] + total
        mean_g = total * (1.0 / total_frames)
        mean_n = with_norm * (1.0 / total_frames) * inv
        sums = jnp.concatenate([colsum[r]] * (channels // 128), axis=1)
        base_part = mean_g * sums
        acc_e[...] += mul * (p_e - base_part - mean_n * (gw[r, :, 0:channels] - mu * sums))
        acc_o[...] += mul * (p_o - base_part - mean_n * (gw[r, :, channels:] - mu * sums))
        acc_t[pl.ds(r, 1), :] = mul * (shift_t - mean_g - mean_n * (pre_t - mu))

    @pl.loop(0, crops // 2)
    def _(r):
        backward(r)

    def peer_x(k):
        return lax.rem(px + k, SIDE)

    def peer_y(k):
        return lax.rem(py + k, SIDE)

    def x_rows(ref, x):
        return jnp.concatenate(
            [ref[pl.ds(pl.multiple_of(i * rz + x * rx, 8), rx), :] for i in range(hz)], axis=0)

    def y_lanes(ref, y):
        return ref[:, pl.ds(pl.multiple_of(128 * y, 128), 128)]

    def at_x(x):
        return (py * SIDE + x, dy)

    def at_y(y):
        return (y * SIDE + px, dy)

    def pair_wait(h):
        send(pair_send.at[h], pair_recv.at[h], pair_ss.at[h], pair_rs.at[h], pair).wait()
        half_sum[h] = half_sum[h] + pair_recv[h].astype(F32)

    def x_copy(k):
        return send(x_send.at[k], x_recv.at[k], plane_ss.at[k], plane_rs.at[k], at_x(peer_x(k)))

    def y_copy(k):
        return send(y_send.at[k], y_recv.at[k], plane_ss.at[4 + k], plane_rs.at[4 + k], at_y(peer_y(k)))

    def y2_copy(k):
        return send(y2_send.at[k], y2_recv.at[k], plane_ss.at[8 + k], plane_rs.at[8 + k], at_y(peer_y(k)))

    def x2_copy(k):
        return send(x2_send.at[k], x2_recv.at[k], plane_ss.at[12 + k], plane_rs.at[12 + k], at_x(peer_x(k)))

    pair_wait(0)
    for k in range(1, SIDE):
        x_send[k] = x_rows(half_sum.at[0], peer_x(k)).astype(BF16)
        x_copy(k).start()
    pair_wait(1)
    for k in range(1, SIDE):
        y_send[k] = y_lanes(half_sum.at[1], peer_y(k)).astype(BF16)
        y_copy(k).start()

    @pl.loop(crops // 2, crops)
    def _(r):
        backward(r)

    tail_grad = lax.dot_general(
        tail_rows, acc_t[...], TN, preferred_element_type=F32, precision=lax.Precision.HIGHEST)
    small[0:10, :] = acc_e[0:10, :] + tail_grad[0:10, :]
    small[0:5, :] = small[0:5, :] + acc_o[5:10, :]
    small[5:10, :] = small[5:10, :] + acc_o[11:16, :]

    units = 8
    for u in range(units):
        s_send[u] = small[8 * (u // 4) : 8 * (u // 4) + 8, 128 * (u % 4) : 128 * (u % 4) + 128]
    lane_of = me * 2 + core
    unit = me // 2
    holder = (lax.rem(me, 2) == 0) & (core == lax.rem(unit, 2))

    @pl.loop(0, units)
    def _(u):
        to_core = lax.rem(u, 2)

        @pl.when((me == 2 * u) & (core == to_core))
        def _():
            s_recv[lane_of] = s_send[u]

        @pl.when((me != 2 * u) | (core != to_core))
        def _():
            send(s_send.at[u], s_recv.at[lane_of], s1_ss.at[u], s1_rs.at[lane_of],
                 (2 * u, 2 * z + to_core)).start()

    xa[...] = x_rows(half_sum.at[0], px)
    ya[...] = y_lanes(half_sum.at[1], py)
    for k in range(1, SIDE):
        x_copy(k).wait()
        xa[...] += x_recv[k].astype(F32)
    for k in range(1, SIDE):
        y2_send[k] = y_lanes(xa, peer_y(k)).astype(BF16)
        y2_copy(k).start()
    for k in range(1, SIDE):
        y_copy(k).wait()
        ya[...] += y_recv[k].astype(F32)
    for k in range(1, SIDE):
        x2_send[k] = x_rows(ya, peer_x(k)).astype(BF16)
        x2_copy(k).start()

    def u_copy(k, slot_at):
        return send(u_val, u_recv.at[slot_at], s2_ss.at[k], s2_rs.at[slot_at], (me, 2 * k + core))

    @pl.when(holder)
    def _():
        @pl.loop(0, 2 * planes)
        def _(i):
            @pl.when(i != lane_of)
            def _():
                send(s_send.at[0], s_recv.at[i], s1_ss.at[0], s1_rs.at[i],
                     (i // 2, 2 * z + lax.rem(i, 2))).wait_recv()

        u_val[...] = jnp.sum(s_recv[...], axis=0)

        @pl.loop(0, depth)
        def _(k):
            @pl.when(k != z)
            def _():
                u_copy(k, z).start()

    part[0:hz] = y_lanes(xa, py).reshape(hz, rx, 128)
    for k in range(1, SIDE):
        y2_copy(k).wait()
        part[0:hz] += y2_recv[k].astype(F32).reshape(hz, rx, 128)
    part[hz:] = x_rows(ya, px).reshape(hz, rx, 128)
    for k in range(1, SIDE):
        x2_copy(k).wait()
        part[hz:] += x2_recv[k].astype(F32).reshape(hz, rx, 128)
    pad = z_send.shape[1] - rx
    padding = [jnp.zeros((zhalf, pad, 128), F32)] if pad else []
    z_send[...] = jnp.concatenate([part[...]] + padding, axis=1).astype(BF16)

    def z_copy(i, slot_at):
        return send(z_send.at[i], z_recv.at[slot_at], z_ss.at[i], z_rs.at[slot_at],
                    (me, 2 * (core * zhalf + i) + core))

    @pl.loop(0, zhalf)
    def _(i):
        @pl.when(core * zhalf + i != z)
        def _():
            z_copy(i, z).start()

    def v_copy(i, slot_at):
        return send(v_val, v_recv.at[slot_at], s3_ss.at[i], s3_rs.at[slot_at],
                    (i // 2, 2 * z + lax.rem(i, 2)))

    @pl.when(holder)
    def _():
        v_val[...] = u_val[...]

        @pl.loop(0, depth)
        def _(k):
            @pl.when(k != z)
            def _():
                u_copy(k, k).wait_recv()
                v_val[...] += u_recv[k]

        v_recv[unit] = v_val[...]

        @pl.loop(0, 2 * planes)
        def _(i):
            @pl.when(i != lane_of)
            def _():
                v_copy(i, unit).start()

    active = z // zhalf == core
    to_core = px // 2
    mine_at = lax.rem(px, 2) * SIDE + py

    def d_copy(p, slot_at):
        return send(full, gathered.at[slot_at], d_ss.at[p], d_rs.at[slot_at], (p, 2 * z + to_core))

    @pl.when(active)
    def _():
        full[...] = part[lax.rem(z, zhalf)]

        @pl.loop(0, depth)
        def _(k):
            @pl.when(k != z)
            def _():
                send(z_send.at[0], z_recv.at[k], z_ss.at[0], z_rs.at[k],
                     (me, 2 * k + core)).wait_recv()
                full[...] += z_recv[k].astype(F32)[0:rx]

        @pl.when(to_core == core)
        def _():
            gathered[mine_at] = full[...]

        @pl.loop(0, planes)
        def _(p):
            @pl.when((p != me) | (to_core != core))
            def _():
                d_copy(p, mine_at).start()

    for u in range(units):
        @pl.when((me != 2 * u) | (core != u % 2))
        def _(u=u):
            v_copy(0, u).wait_recv()
    for u in range(units):
        cols = slice(128 * (u % 4), 128 * (u % 4) + 128)
        if u < 4:
            first_out[0:8, cols] = v_recv[u]
        else:
            first_out[8:10, cols] = v_recv[u, 0:2]
            norm_out[:, cols] = v_recv[u, 2:4]

    owner = z // zhalf
    for i in range(2):
        for y in range(SIDE):
            sender = y * SIDE + 2 * core + i

            @pl.when((sender != me) | (owner != core))
            def _(i=i, y=y):
                send(full, gathered.at[i * SIDE + y], d_ss.at[0], d_rs.at[i * SIDE + y],
                     (me, dy + 1 - 2 * core)).wait_recv()
            second_out[rx * i : rx * i + rx, 128 * y : 128 * y + 128] = gathered[i * SIDE + y]

    @pl.loop(0, units)
    def _(u):
        @pl.when((me != 2 * u) | (core != lax.rem(u, 2)))
        def _():
            send(s_send.at[u], s_recv.at[lane_of], s1_ss.at[u], s1_rs.at[lane_of],
                 (2 * u, 2 * z + lax.rem(u, 2))).wait_send()

    @pl.when(holder)
    def _():
        @pl.loop(0, depth)
        def _(k):
            @pl.when(k != z)
            def _():
                u_copy(k, z).wait_send()

        @pl.loop(0, 2 * planes)
        def _(i):
            @pl.when(i != lane_of)
            def _():
                v_copy(i, unit).wait_send()

    @pl.loop(0, zhalf)
    def _(i):
        @pl.when(core * zhalf + i != z)
        def _():
            z_copy(i, z).wait_send()

    @pl.when(active)
    def _():
        @pl.loop(0, planes)
        def _(p):
            @pl.when((p != me) | (to_core != core))
            def _():
                d_copy(p, mine_at).wait_send()


def on_device(audio, counts, cotangent, conv_first, norm_gain, norm_bias, conv_second):
    planes = lax.axis_size("dx")
    groups = lax.axis_size("dy")
    depth = groups // 2
    crops, frames, channels = cotangent.shape[1:]
    rows_all = conv_second.shape[0]
    scale = 1.0 / math.sqrt(planes * groups * crops * frames)
    zhalf = depth // 2
    hz = zhalf // 2
    half_rows = rows_all // 2
    hrows = half_rows // 2
    rx = rows_all // depth // SIDE
    rpad = -(-rx // 16) * 16
    vm = pltpu.VMEM
    dma = pltpu.SemaphoreType.DMA
    scratch = [
        vm(audio.shape, BF16), vm(cotangent.shape, BF16), vm(conv_first.shape, BF16),
        vm((channels,), F32), vm((channels,), F32), vm(conv_second.shape, BF16), dma((6,)),
        vm((640, 640), BF16), vm((8, 16, 256), F32), vm((planes, 1, 128), jnp.int32),
        vm((planes, 16, 256), BF16), vm((planes, 16, 256), BF16),
        vm((16 * crops, 256), F32), vm((16 * crops, 256), BF16),
        vm((16, 2 * channels), F32), vm((128, channels), F32),
        vm((crops, 192, 2 * channels), BF16), vm((crops, 16, 2 * channels), F32),
        vm((crops, 8, channels), F32), vm((crops, 16, 128), F32),
        vm((2, crops * frames, half_rows), BF16), vm((crops * frames, channels), BF16),
        vm((crops, frames, channels), F32), vm((crops, frames, channels), F32),
        vm((crops, 1, channels), F32), vm((frames + 8, channels), F32),
        vm((frames + 8, channels), F32),
        vm((2, hrows, channels), F32), vm((2, hrows, channels), BF16),
        vm((2, hrows, channels), BF16),
        vm((SIDE, hz * rx, channels), BF16), vm((SIDE, hz * rx, channels), BF16),
        vm((SIDE, hrows, 128), BF16), vm((SIDE, hrows, 128), BF16),
        vm((hz * rx, channels), F32), vm((hrows, 128), F32),
        vm((SIDE, hz * rx, 128), BF16), vm((SIDE, hz * rx, 128), BF16),
        vm((SIDE, hz * rx, 128), BF16), vm((SIDE, hz * rx, 128), BF16),
        vm((zhalf, rx, 128), F32), vm((zhalf, rpad, 128), BF16), vm((depth, rpad, 128), BF16),
        vm((rx, 128), F32), vm((8, rx, 128), F32),
        vm((16, channels), F32), vm((16, channels), F32), vm((8, channels), F32),
        vm((16, channels), F32), vm((8, 8, 128), F32), vm((2 * planes, 8, 128), F32),
        vm((8, 128), F32), vm((depth, 8, 128), F32), vm((8, 128), F32), vm((8, 8, 128), F32),
        dma((planes,)), dma((planes,)), dma((planes,)), dma((planes,)), dma((2,)), dma((2,)),
        dma((16,)), dma((16,)), dma((zhalf,)), dma((depth,)), dma((planes,)), dma((8,)),
        dma((8,)), dma((2 * planes,)), dma((depth,)), dma((depth,)), dma((2 * planes,)), dma((8,)),
    ]
    hbm = pl.BlockSpec(memory_space=pl.ANY)
    vmem = pl.BlockSpec(memory_space=pltpu.VMEM)
    return tuple(pl.pallas_call(
        functools.partial(kernel, planes, depth, scale),
        out_shape=[
            jax.ShapeDtypeStruct(conv_first.shape, F32),
            jax.ShapeDtypeStruct((2, channels), F32),
            jax.ShapeDtypeStruct((rows_all // groups, channels), F32),
        ],
        in_specs=[hbm, pl.BlockSpec(memory_space=pltpu.SMEM), hbm, hbm, hbm, hbm, hbm],
        out_specs=[vmem] * 3,
        scratch_shapes=scratch,
        compiler_params=pltpu.CompilerParams(
            collective_id=0, has_side_effects=True, vmem_limit_bytes=50 * 2**20),
    )(audio, counts, cotangent, conv_first, norm_gain, norm_bias, conv_second))


def solution(mesh):
    in_specs = (P("dy", "dx", None), P("dy", "dx"), P("dy", "dx", None, None), P(), P(), P(), P())
    out_specs = (P(), P(), P("dy", None))
    return jax.shard_map(
        on_device, mesh=mesh, in_specs=in_specs, out_specs=out_specs, check_vma=False
    )
```

time: 584 us -> 71.5 us (0.12)
  waiting for transfers between devices: 346 us -> 0 us
  blocking collectives: 148 us -> 0 us
  Pallas kernels: 0 us -> 62.5 us
  local copies, waits for them, and re-layouts: 47.7 us -> 7.34 us
  between operations: 15 us -> 1.3 us
  matrix products: 13.3 us -> 0 us
  other arithmetic: 12.5 us -> 0 us
    psum x1 -> x0, waiting for transfers between devices: 346 us -> none  [on_device(): lax.psum((grad_first, grad_gains, grad_second), ('dx', 'dy'))]
    psum x1 -> x0, blocking collectives: 117 us -> none  [on_device(): lax.psum((grad_first, grad_gains, grad_second), ('dx', 'dy'))]
    pallas_call x0 -> x1, Pallas kernels: none -> 62.5 us  [on_device(): pl.pallas_call(functools.partial(kernel, planes, depth, scale), out_shape...]
    slice x5 -> x0, local copies, waits for them, and re-layouts: 18.7 us -> none  [the longest x1 11.7 us: forward_backward(): third_tap = hidden[:, 2::2]]
    all_gather x1 -> x0, blocking collectives: 17.5 us -> none  [on_device(): everything = lax.all_gather(audio, 'dx', axis=1, tiled=True)[0]]
    squeeze x1 -> x0, blocking collectives: 13.9 us -> none  [on_device(): all_counts = lax.all_gather(counts, 'dx', axis=1, tiled=True)[0]]
    dot_general x5 -> x0, matrix products: 13.3 us -> none  [the longest x1 5.05 us: forward_backward(): jnp.dot(second_rows, conv_second, preferred_element_type=jnp.float32)]
    reshape x7 -> x0, local copies, waits for them, and re-layouts: 12.5 us -> none  [the longest x1 6.08 us: forward_backward(): late_tap = jnp.stack([grad_cols[:, :, 2 * channels:], jnp.zeros((batch_si...]
  transfers between devices with their start and end apart: 1 -> 0, of which waited for: 1 -> 0; matrix products, arithmetic and copies ran while one was open for 5% -> 0% of each run, Pallas kernels for 0% -> 0%
where the time goes in v1:
time: 71.5 us; the launch traced here: 71.2 us
  Pallas kernels  62.5 us (87%)
  local copies, waits for them, and re-layouts  7.34 us (10%)
  between operations  1.3 us (2%)
    pallas_call x1, Pallas kernels, on_device(): pl.pallas_call(functools.partial(kernel, planes, depth, scale), out_shape...  62.5 us
    unnamed x15, local copies, waits for them, and re-layouts  7.34 us

profile of v1, /device:TPU:1, one launch (start us, length us, event | category | flops | bytes accessed | tf_op | source)
XLA Modules:
  0.0 71.2 jit_solution(8830793114352914116)
XLA Ops:
  1.3 0.0 copy-start
  1.3 1.4 %copy-done = bf16[1536,512]{1,0:T(8,128)(2,1)S(1)} copy-done((bf16[1536,512]{1,0:T(8,128)(2,1)S(1)}, bf16[1536,512]{1,0:T(8,128)(2,1)}, u32[]{:S(2)}) %copy-start) | copy-done | bytes 1572888
  2.7 0.0 copy-start.1
  2.7 1.2 %copy-done.1 = bf16[1,4,256,512]{3,2,1,0:T(8,128)(2,1)S(1)} copy-done((bf16[1,4,256,512]{3,2,1,0:T(8,128)(2,1)S(1)}, bf16[1,4,256,512]{3,2,1,0:T(8,128)(2,1)}, u32[]{:S(2)}) %copy-start.1) | copy-done | bytes 1048600
  3.9 0.0 copy-start.2
  3.9 0.8 %copy-done.2 = bf16[1,8,2570]{2,1,0:T(8,128)(2,1)S(1)} copy-done((bf16[1,8,2570]{2,1,0:T(8,128)(2,1)S(1)}, bf16[1,8,2570]{2,1,0:T(8,128)(2,1)}, u32[]{:S(2)}) %copy-start.2) | copy-done | bytes 41144
  4.7 0.0 copy-start.3
  4.7 0.7 %copy-done.3 = bf16[10,512]{1,0:T(8,128)(2,1)S(1)} copy-done((bf16[10,512]{1,0:T(8,128)(2,1)S(1)}, bf16[10,512]{1,0:T(8,128)(2,1)}, u32[]{:S(2)}) %copy-start.3) | copy-done | bytes 10264
  5.4 0.0 copy-start.4
  5.4 0.7 copy-done.4
  6.1 0.0 copy-start.5
  6.1 0.7 copy-done.5
  6.8 62.5 %shard_map.94 = (f32[10,512]{1,0:T(8,128)S(1)}, f32[2,512]{1,0:T(2,128)S(1)}, f32[48,512]{1,0:T(8,128)S(1)}) custom-call(bf16[1,8,2570]{2,1,0:T(8,128)(2,1)S(1)} %copy-done.2, s32[1,1]{1,0:T(1,128)S(6)} %copy.13.counts_ref, bf16[1,4,256,512]{3,2,1,0:T(8,128)(2,1)S(1)} %copy-done.1, bf16[10,512]{1,0:T(8,128)(2,1)S(1)} %copy-done.3, f32[512]{0:T(512)S(1)} %copy-done.4, ...), custom_call_target="tpu_custom_call" | custom-call | tf_op jit(solution)/shard_map/pallas_call | solution.py:606
  69.3 0.6 copy.14
  69.9 0.6 copy.15
  70.5 0.6 copy.16
Async XLA Ops:
  1.3 1.4 %copy-start = (bf16[1536,512]{1,0:T(8,128)(2,1)S(1)}, bf16[1536,512]{1,0:T(8,128)(2,1)}, u32[]{:S(2)}) copy-start(bf16[1536,512]{1,0:T(8,128)(2,1)} %w2_hbm.1) | copy-start | bytes 4718596
  2.7 1.2 %copy-start.1 = (bf16[1,4,256,512]{3,2,1,0:T(8,128)(2,1)S(1)}, bf16[1,4,256,512]{3,2,1,0:T(8,128)(2,1)}, u32[]{:S(2)}) copy-start(bf16[1,4,256,512]{3,2,1,0:T(8,128)(2,1)} %cot_hbm.1) | copy-start | bytes 3145732
  3.9 0.8 %copy-start.2 = (bf16[1,8,2570]{2,1,0:T(8,128)(2,1)S(1)}, bf16[1,8,2570]{2,1,0:T(8,128)(2,1)}, u32[]{:S(2)}) copy-start(bf16[1,8,2570]{2,1,0:T(8,128)(2,1)} %audio_hbm.1) | copy-start | bytes 123364
  4.7 0.7 %copy-start.3 = (bf16[10,512]{1,0:T(8,128)(2,1)S(1)}, bf16[10,512]{1,0:T(8,128)(2,1)}, u32[]{:S(2)}) copy-start(bf16[10,512]{1,0:T(8,128)(2,1)} %w1_hbm.1) | copy-start | bytes 30724
  5.4 0.7 copy-start.4
  6.1 0.7 copy-start.5

commit v2 on v1

--- a/solution.py
+++ b/solution.py
@@ -46,14 +46,12 @@
 
 def kernel(
     planes, depth, scale,
-    audio_hbm, counts_ref, cot_hbm, w1_hbm, gain_hbm, bias_hbm, w2_hbm,
+    audio_hbm, counts_hbm, cot_hbm, w1_hbm, gain_hbm, bias_hbm, w2_hbm,
     first_out, norm_out, second_out,
-    audio, cot, w1, gain_ref, bias_ref, w2, load_sem,
+    audio, counts_ref, cot, w1, gain_ref, bias_ref, w2, load_sem,
     perm, zbuf, cnt_all, crop_send, crop_recv, xf, xp, weo, wpad, waug, gw, stat, colsum,
     hid, grows, slope_e, slope_o, slope_t, hshift, dshift,
-    half_sum, pair_send, pair_recv,
-    x_send, x_recv, y_send, y_recv, xa, ya, x2_send, x2_recv, y2_send, y2_recv,
-    part, z_send, z_recv, full, gathered,
+    half_sum, pair_send, pair_recv, p_send, p_recv, part, z_send, z_recv, full, gathered,
     acc_e, acc_o, acc_t, small, s_send, s_recv, u_val, u_recv, v_val, v_recv,
     cnt_ss, cnt_rs, crop_ss, crop_rs, pair_ss, pair_rs, plane_ss, plane_rs,
     z_ss, z_rs, d_ss, d_rs, s1_ss, s1_rs, s2_ss, s2_rs, s3_ss, s3_rs,
@@ -86,7 +84,7 @@
         pltpu.make_async_copy(src, dst, load_sem.at[i])
         for i, (src, dst) in enumerate(
             ((audio_hbm, audio), (w1_hbm, w1), (gain_hbm, gain_ref), (bias_hbm, bias_ref),
-             (w2_hbm, w2), (cot_hbm, cot))
+             (w2_hbm, w2), (cot_hbm, cot), (counts_hbm, counts_ref))
         )
     ]
     for load in loads:
@@ -113,6 +111,7 @@
     for i in range(5):
         block = rows_of((128, 640)) + 128 * i
         perm[pl.ds(128 * i, 128), :] = jnp.where(block == sample, 1.0, 0.0).astype(BF16)
+    loads[6].wait()
     cnt_all[me] = jnp.full((1, 128), counts_ref[0, 0], jnp.int32)
 
     loads[0].wait()
@@ -281,6 +280,25 @@
     for h in range(2):
         half_sum[h] = dot(hid[core, :, h * hrows : (h + 1) * hrows], grows[...], TN)
 
+    def p_copy(h, k, slot, slot_at, where):
+        return send(p_send.at[h, slot], p_recv.at[h, slot_at], plane_ss.at[h, k], plane_rs.at[h, k],
+                    (where, dy))
+
+    for h in range(2):
+        send(pair_send.at[h], pair_recv.at[h], pair_ss.at[h], pair_rs.at[h], pair).wait()
+        half_sum[h] = half_sum[h] + pair_recv[h].astype(F32)
+        for p in range(planes):
+            lanes = slice(128 * (p // SIDE), 128 * (p // SIDE) + 128)
+            first = (p % SIDE) * rx
+            p_send[h, p] = jnp.concatenate(
+                [half_sum[h, i * rz + first : i * rz + first + rx, lanes] for i in range(hz)], axis=0
+            ).astype(BF16)
+
+        @pl.loop(1, planes)
+        def _(k):
+            to = lax.rem(me + k, planes)
+            p_copy(h, k, to, me, to).start()
+
     acc_e[...] = jnp.zeros_like(acc_e)
     acc_o[...] = jnp.zeros_like(acc_o)
     acc_t[...] = jnp.zeros_like(acc_t)
@@ -311,55 +329,7 @@
         acc_o[...] += mul * (p_o - base_part - mean_n * (gw[r, :, channels:] - mu * sums))
         acc_t[pl.ds(r, 1), :] = mul * (shift_t - mean_g - mean_n * (pre_t - mu))
 
-    @pl.loop(0, crops // 2)
-    def _(r):
-        backward(r)
-
-    def peer_x(k):
-        return lax.rem(px + k, SIDE)
-
-    def peer_y(k):
-        return lax.rem(py + k, SIDE)
-
-    def x_rows(ref, x):
-        return jnp.concatenate(
-            [ref[pl.ds(pl.multiple_of(i * rz + x * rx, 8), rx), :] for i in range(hz)], axis=0)
-
-    def y_lanes(ref, y):
-        return ref[:, pl.ds(pl.multiple_of(128 * y, 128), 128)]
-
-    def at_x(x):
-        return (py * SIDE + x, dy)
-
-    def at_y(y):
-        return (y * SIDE + px, dy)
-
-    def pair_wait(h):
-        send(pair_send.at[h], pair_recv.at[h], pair_ss.at[h], pair_rs.at[h], pair).wait()
-        half_sum[h] = half_sum[h] + pair_recv[h].astype(F32)
-
-    def x_copy(k):
-        return send(x_send.at[k], x_recv.at[k], plane_ss.at[k], plane_rs.at[k], at_x(peer_x(k)))
-
-    def y_copy(k):
-        return send(y_send.at[k], y_recv.at[k], plane_ss.at[4 + k], plane_rs.at[4 + k], at_y(peer_y(k)))
-
-    def y2_copy(k):
-        return send(y2_send.at[k], y2_recv.at[k], plane_ss.at[8 + k], plane_rs.at[8 + k], at_y(peer_y(k)))
-
-    def x2_copy(k):
-        return send(x2_send.at[k], x2_recv.at[k], plane_ss.at[12 + k], plane_rs.at[12 + k], at_x(peer_x(k)))
-
-    pair_wait(0)
-    for k in range(1, SIDE):
-        x_send[k] = x_rows(half_sum.at[0], peer_x(k)).astype(BF16)
-        x_copy(k).start()
-    pair_wait(1)
-    for k in range(1, SIDE):
-        y_send[k] = y_lanes(half_sum.at[1], peer_y(k)).astype(BF16)
-        y_copy(k).start()
-
-    @pl.loop(crops // 2, crops)
+    @pl.loop(0, crops)
     def _(r):
         backward(r)
 
@@ -389,20 +359,33 @@
             send(s_send.at[u], s_recv.at[lane_of], s1_ss.at[u], s1_rs.at[lane_of],
                  (2 * u, 2 * z + to_core)).start()
 
-    xa[...] = x_rows(half_sum.at[0], px)
-    ya[...] = y_lanes(half_sum.at[1], py)
-    for k in range(1, SIDE):
-        x_copy(k).wait()
-        xa[...] += x_recv[k].astype(F32)
-    for k in range(1, SIDE):
-        y2_send[k] = y_lanes(xa, peer_y(k)).astype(BF16)
-        y2_copy(k).start()
-    for k in range(1, SIDE):
-        y_copy(k).wait()
-        ya[...] += y_recv[k].astype(F32)
-    for k in range(1, SIDE):
-        x2_send[k] = x_rows(ya, peer_x(k)).astype(BF16)
-        x2_copy(k).start()
+    mine_rows = pl.multiple_of(px * rx, 8)
+    mine_lanes = pl.ds(pl.multiple_of(128 * py, 128), 128)
+    pad = z_send.shape[1] - rx
+
+    def z_copy(i, slot_at):
+        return send(z_send.at[i], z_recv.at[slot_at], z_ss.at[i], z_rs.at[slot_at],
+                    (me, 2 * (core * zhalf + i) + core))
+
+    for h in range(2):
+        own = jnp.concatenate(
+            [half_sum[h, pl.ds(i * rz + mine_rows, rx), mine_lanes] for i in range(hz)], axis=0)
+
+        def add(k, total):
+            frm = lax.rem(me - k + planes, planes)
+            p_copy(h, k, frm, frm, frm).wait()
+            return total + p_recv[h, frm].astype(F32)
+
+        own = lax.fori_loop(1, planes, add, own).reshape(hz, rx, 128)
+        part[h * hz : h * hz + hz] = own
+        padding = [jnp.zeros((hz, pad, 128), F32)] if pad else []
+        z_send[h * hz : h * hz + hz] = jnp.concatenate([own] + padding, axis=1).astype(BF16)
+
+        @pl.loop(h * hz, h * hz + hz)
+        def _(i):
+            @pl.when(core * zhalf + i != z)
+            def _():
+                z_copy(i, z).start()
 
     def u_copy(k, slot_at):
         return send(u_val, u_recv.at[slot_at], s2_ss.at[k], s2_rs.at[slot_at], (me, 2 * k + core))
@@ -423,28 +406,6 @@
             @pl.when(k != z)
             def _():
                 u_copy(k, z).start()
-
-    part[0:hz] = y_lanes(xa, py).reshape(hz, rx, 128)
-    for k in range(1, SIDE):
-        y2_copy(k).wait()
-        part[0:hz] += y2_recv[k].astype(F32).reshape(hz, rx, 128)
-    part[hz:] = x_rows(ya, px).reshape(hz, rx, 128)
-    for k in range(1, SIDE):
-        x2_copy(k).wait()
-        part[hz:] += x2_recv[k].astype(F32).reshape(hz, rx, 128)
-    pad = z_send.shape[1] - rx
-    padding = [jnp.zeros((zhalf, pad, 128), F32)] if pad else []
-    z_send[...] = jnp.concatenate([part[...]] + padding, axis=1).astype(BF16)
-
-    def z_copy(i, slot_at):
-        return send(z_send.at[i], z_recv.at[slot_at], z_ss.at[i], z_rs.at[slot_at],
-                    (me, 2 * (core * zhalf + i) + core))
-
-    @pl.loop(0, zhalf)
-    def _(i):
-        @pl.when(core * zhalf + i != z)
-        def _():
-            z_copy(i, z).start()
 
     def v_copy(i, slot_at):
         return send(v_val, v_recv.at[slot_at], s3_ss.at[i], s3_rs.at[slot_at],
@@ -573,8 +534,8 @@
     vm = pltpu.VMEM
     dma = pltpu.SemaphoreType.DMA
     scratch = [
-        vm(audio.shape, BF16), vm(cotangent.shape, BF16), vm(conv_first.shape, BF16),
-        vm((channels,), F32), vm((channels,), F32), vm(conv_second.shape, BF16), dma((6,)),
+        vm(audio.shape, BF16), pltpu.SMEM((1, 1), jnp.int32), vm(cotangent.shape, BF16), vm(conv_first.shape, BF16),
+        vm((channels,), F32), vm((channels,), F32), vm(conv_second.shape, BF16), dma((7,)),
         vm((640, 640), BF16), vm((8, 16, 256), F32), vm((planes, 1, 128), jnp.int32),
         vm((planes, 16, 256), BF16), vm((planes, 16, 256), BF16),
         vm((16 * crops, 256), F32), vm((16 * crops, 256), BF16),
@@ -587,35 +548,52 @@
         vm((frames + 8, channels), F32),
         vm((2, hrows, channels), F32), vm((2, hrows, channels), BF16),
         vm((2, hrows, channels), BF16),
-        vm((SIDE, hz * rx, channels), BF16), vm((SIDE, hz * rx, channels), BF16),
-        vm((SIDE, hrows, 128), BF16), vm((SIDE, hrows, 128), BF16),
-        vm((hz * rx, channels), F32), vm((hrows, 128), F32),
-        vm((SIDE, hz * rx, 128), BF16), vm((SIDE, hz * rx, 128), BF16),
-        vm((SIDE, hz * rx, 128), BF16), vm((SIDE, hz * rx, 128), BF16),
+        vm((2, planes, hz * rx, 128), BF16), vm((2, planes, hz * rx, 128), BF16),
         vm((zhalf, rx, 128), F32), vm((zhalf, rpad, 128), BF16), vm((depth, rpad, 128), BF16),
         vm((rx, 128), F32), vm((8, rx, 128), F32),
         vm((16, channels), F32), vm((16, channels), F32), vm((8, channels), F32),
         vm((16, channels), F32), vm((8, 8, 128), F32), vm((2 * planes, 8, 128), F32),
         vm((8, 128), F32), vm((depth, 8, 128), F32), vm((8, 128), F32), vm((8, 8, 128), F32),
         dma((planes,)), dma((planes,)), dma((planes,)), dma((planes,)), dma((2,)), dma((2,)),
-        dma((16,)), dma((16,)), dma((zhalf,)), dma((depth,)), dma((planes,)), dma((8,)),
+        dma((2, planes)), dma((2, planes)), dma((zhalf,)), dma((depth,)), dma((planes,)), dma((8,)),
         dma((8,)), dma((2 * planes,)), dma((depth,)), dma((depth,)), dma((2 * planes,)), dma((8,)),
     ]
-    hbm = pl.BlockSpec(memory_space=pl.ANY)
+    hbm = pl.BlockSpec(memory_space=pltpu.HBM)
     vmem = pl.BlockSpec(memory_space=pltpu.VMEM)
-    return tuple(pl.pallas_call(
+    outs = pl.pallas_call(
         functools.partial(kernel, planes, depth, scale),
         out_shape=[
             jax.ShapeDtypeStruct(conv_first.shape, F32),
             jax.ShapeDtypeStruct((2, channels), F32),
             jax.ShapeDtypeStruct((rows_all // groups, channels), F32),
         ],
-        in_specs=[hbm, pl.BlockSpec(memory_space=pltpu.SMEM), hbm, hbm, hbm, hbm, hbm],
+        in_specs=[hbm, hbm, hbm, hbm, hbm, hbm, hbm],
         out_specs=[vmem] * 3,
         scratch_shapes=scratch,
         compiler_params=pltpu.CompilerParams(
-            collective_id=0, has_side_effects=True, vmem_limit_bytes=50 * 2**20),
-    )(audio, counts, cotangent, conv_first, norm_gain, norm_bias, conv_second))
+            collective_id=0, has_side_effects=True, vmem_limit_bytes=63 * 2**20),
+    )(audio, counts, cotangent, conv_first, norm_gain, norm_bias, conv_second)
+
+    def place(*refs):
+        ins, results, held, sems = refs[0:3], refs[3:6], refs[6:9], refs[9]
+        reads = [pltpu.make_async_copy(ins[i], held[i], sems.at[i]) for i in range(3)]
+        writes = [pltpu.make_async_copy(held[i], results[i], sems.at[3 + i]) for i in range(3)]
+        for read in reads:
+            read.start()
+        for read, write in zip(reads, writes):
+            read.wait()
+            write.start()
+        for write in writes:
+            write.wait()
+
+    return tuple(pl.pallas_call(
+        place,
+        out_shape=[jax.ShapeDtypeStruct(out.shape, out.dtype) for out in outs],
+        in_specs=[hbm] * 3,
+        out_specs=[pl.BlockSpec(memory_space=pltpu.HBM)] * 3,
+        scratch_shapes=[vm(out.shape, F32) for out in outs] + [dma((6,))],
+        compiler_params=pltpu.CompilerParams(vmem_limit_bytes=63 * 2**20),
+    )(*outs))
 
 
 def solution(mesh):

time: 71.5 us -> 65.9 us (0.922)
  local copies, waits for them, and re-layouts: 7.34 us -> 0 us
  Pallas kernels: 62.5 us -> 64.5 us
    unnamed x15 -> x0, local copies, waits for them, and re-layouts: 7.34 us -> none
    pallas_call x0 -> x1, Pallas kernels: none -> 1.61 us  [on_device(): pl.pallas_call(place, out_shape=[jax.ShapeDtypeStruct(out.shape, out.dtyp...]
where the time goes in v2:
time: 65.9 us; the launch traced here: 65.7 us
  Pallas kernels  64.5 us (98%)
  between operations  1.29 us (2%)
    pallas_call x1, Pallas kernels, on_device(): pl.pallas_call(functools.partial(kernel, planes, depth, scale), out_shape...  62.8 us
    pallas_call x1, Pallas kernels, on_device(): pl.pallas_call(place, out_shape=[jax.ShapeDtypeStruct(out.shape, out.dtyp...  1.61 us

profile of v2, /device:TPU:1, one launch (start us, length us, event | category | flops | bytes accessed | tf_op | source)
XLA Modules:
  0.0 65.7 jit_solution(9261564218883030981)
XLA Ops:
  1.3 62.8 %shard_map.94 = (f32[10,512]{1,0:T(8,128)}, f32[2,512]{1,0:T(2,128)}, f32[48,512]{1,0:T(8,128)}) custom-call(bf16[1,8,2570]{2,1,0:T(8,128)(2,1)} %audio_hbm.1, s32[1,1]{1,0:T(1,128)S(6)} %copy.10.counts_hbm, bf16[1,4,256,512]{3,2,1,0:T(8,128)(2,1)} %cot_hbm.1, bf16[10,512]{1,0:T(8,128)(2,1)} %w1_hbm.1, f32[512]{0:T(512)} %gain_hbm.1, f32[512]{0:T(512)} %bias_hbm.1, ...), custom_call_target="tpu_custom_call" | custom-call | tf_op jit(solution)/shard_map/pallas_call | solution.py:563
  64.1 1.6 %shard_map.95 = (f32[10,512]{1,0:T(8,128)}, f32[2,512]{1,0:T(2,128)}, f32[48,512]{1,0:T(8,128)}) custom-call(f32[10,512]{1,0:T(8,128)} %get-tuple-element.6.refs_0_, f32[2,512]{1,0:T(2,128)} %get-tuple-element.7.refs_1_, f32[48,512]{1,0:T(8,128)} %get-tuple-element.8.refs_2_), custom_call_target="tpu_custom_call" | custom-call | tf_op jit(solution)/shard_map/pallas_call | solution.py:589

commit v3 on v2

--- a/solution.py
+++ b/solution.py
@@ -46,9 +46,9 @@
 
 def kernel(
     planes, depth, scale,
-    audio_hbm, counts_hbm, cot_hbm, w1_hbm, gain_hbm, bias_hbm, w2_hbm,
+    audio_hbm, counts_ref, cot_hbm, w1_hbm, gain_hbm, bias_hbm, w2_hbm,
     first_out, norm_out, second_out,
-    audio, counts_ref, cot, w1, gain_ref, bias_ref, w2, load_sem,
+    audio, cot, w1, gain_ref, bias_ref, w2, load_sem,
     perm, zbuf, cnt_all, crop_send, crop_recv, xf, xp, weo, wpad, waug, gw, stat, colsum,
     hid, grows, slope_e, slope_o, slope_t, hshift, dshift,
     half_sum, pair_send, pair_recv, p_send, p_recv, part, z_send, z_recv, full, gathered,
@@ -84,7 +84,7 @@
         pltpu.make_async_copy(src, dst, load_sem.at[i])
         for i, (src, dst) in enumerate(
             ((audio_hbm, audio), (w1_hbm, w1), (gain_hbm, gain_ref), (bias_hbm, bias_ref),
-             (w2_hbm, w2), (cot_hbm, cot), (counts_hbm, counts_ref))
+             (w2_hbm, w2), (cot_hbm, cot))
         )
     ]
     for load in loads:
@@ -111,8 +111,7 @@
     for i in range(5):
         block = rows_of((128, 640)) + 128 * i
         perm[pl.ds(128 * i, 128), :] = jnp.where(block == sample, 1.0, 0.0).astype(BF16)
-    loads[6].wait()
-    cnt_all[me] = jnp.full((1, 128), counts_ref[0, 0], jnp.int32)
+    cnt_all[me] = counts_ref[...]
 
     loads[0].wait()
     blocks = jnp.concatenate(
@@ -242,8 +241,7 @@
     quarter = channels // 2
     xt_parts = [xt[128 * i : 128 * i + 128] for i in range(frames // 128)]
 
-    @pl.loop(0, crops)
-    def _(r):
+    for r in range(crops):
         base = pl.multiple_of(r * frames, frames)
         tail = stat[r, 4:5]
         cdf, slope = gelu_parts(tail)
@@ -277,14 +275,16 @@
         theirs = dot(hid[1 - core, :, h * hrows : (h + 1) * hrows], grows[...], TN)
         pair_send[h] = theirs.astype(BF16)
         send(pair_send.at[h], pair_recv.at[h], pair_ss.at[h], pair_rs.at[h], pair).start()
-    for h in range(2):
-        half_sum[h] = dot(hid[core, :, h * hrows : (h + 1) * hrows], grows[...], TN)
+        if h == 0:
+            half_sum[0] = dot(hid[core, :, 0:hrows], grows[...], TN)
 
     def p_copy(h, k, slot, slot_at, where):
         return send(p_send.at[h, slot], p_recv.at[h, slot_at], plane_ss.at[h, k], plane_rs.at[h, k],
                     (where, dy))
 
     for h in range(2):
+        if h == 1:
+            half_sum[1] = dot(hid[core, :, hrows:], grows[...], TN)
         send(pair_send.at[h], pair_recv.at[h], pair_ss.at[h], pair_rs.at[h], pair).wait()
         half_sum[h] = half_sum[h] + pair_recv[h].astype(F32)
         for p in range(planes):
@@ -329,8 +329,7 @@
         acc_o[...] += mul * (p_o - base_part - mean_n * (gw[r, :, channels:] - mu * sums))
         acc_t[pl.ds(r, 1), :] = mul * (shift_t - mean_g - mean_n * (pre_t - mu))
 
-    @pl.loop(0, crops)
-    def _(r):
+    for r in range(crops):
         backward(r)
 
     tail_grad = lax.dot_general(
@@ -359,34 +358,6 @@
             send(s_send.at[u], s_recv.at[lane_of], s1_ss.at[u], s1_rs.at[lane_of],
                  (2 * u, 2 * z + to_core)).start()
 
-    mine_rows = pl.multiple_of(px * rx, 8)
-    mine_lanes = pl.ds(pl.multiple_of(128 * py, 128), 128)
-    pad = z_send.shape[1] - rx
-
-    def z_copy(i, slot_at):
-        return send(z_send.at[i], z_recv.at[slot_at], z_ss.at[i], z_rs.at[slot_at],
-                    (me, 2 * (core * zhalf + i) + core))
-
-    for h in range(2):
-        own = jnp.concatenate(
-            [half_sum[h, pl.ds(i * rz + mine_rows, rx), mine_lanes] for i in range(hz)], axis=0)
-
-        def add(k, total):
-            frm = lax.rem(me - k + planes, planes)
-            p_copy(h, k, frm, frm, frm).wait()
-            return total + p_recv[h, frm].astype(F32)
-
-        own = lax.fori_loop(1, planes, add, own).reshape(hz, rx, 128)
-        part[h * hz : h * hz + hz] = own
-        padding = [jnp.zeros((hz, pad, 128), F32)] if pad else []
-        z_send[h * hz : h * hz + hz] = jnp.concatenate([own] + padding, axis=1).astype(BF16)
-
-        @pl.loop(h * hz, h * hz + hz)
-        def _(i):
-            @pl.when(core * zhalf + i != z)
-            def _():
-                z_copy(i, z).start()
-
     def u_copy(k, slot_at):
         return send(u_val, u_recv.at[slot_at], s2_ss.at[k], s2_rs.at[slot_at], (me, 2 * k + core))
 
@@ -406,6 +377,34 @@
             @pl.when(k != z)
             def _():
                 u_copy(k, z).start()
+
+    mine_rows = pl.multiple_of(px * rx, 8)
+    mine_lanes = pl.ds(pl.multiple_of(128 * py, 128), 128)
+    pad = z_send.shape[1] - rx
+
+    def z_copy(i, slot_at):
+        return send(z_send.at[i], z_recv.at[slot_at], z_ss.at[i], z_rs.at[slot_at],
+                    (me, 2 * (core * zhalf + i) + core))
+
+    for h in range(2):
+        own = jnp.concatenate(
+            [half_sum[h, pl.ds(i * rz + mine_rows, rx), mine_lanes] for i in range(hz)], axis=0)
+
+        def add(k, total):
+            frm = lax.rem(me - k + planes, planes)
+            p_copy(h, k, frm, frm, frm).wait()
+            return total + p_recv[h, frm].astype(F32)
+
+        own = lax.fori_loop(1, planes, add, own).reshape(hz, rx, 128)
+        part[h * hz : h * hz + hz] = own
+        padding = [jnp.zeros((hz, pad, 128), F32)] if pad else []
+        z_send[h * hz : h * hz + hz] = jnp.concatenate([own] + padding, axis=1).astype(BF16)
+
+        @pl.loop(h * hz, h * hz + hz)
+        def _(i):
+            @pl.when(core * zhalf + i != z)
+            def _():
+                z_copy(i, z).start()
 
     def v_copy(i, slot_at):
         return send(v_val, v_recv.at[slot_at], s3_ss.at[i], s3_rs.at[slot_at],
@@ -534,8 +533,8 @@
     vm = pltpu.VMEM
     dma = pltpu.SemaphoreType.DMA
     scratch = [
-        vm(audio.shape, BF16), pltpu.SMEM((1, 1), jnp.int32), vm(cotangent.shape, BF16), vm(conv_first.shape, BF16),
-        vm((channels,), F32), vm((channels,), F32), vm(conv_second.shape, BF16), dma((7,)),
+        vm(audio.shape, BF16), vm(cotangent.shape, BF16), vm(conv_first.shape, BF16),
+        vm((channels,), F32), vm((channels,), F32), vm(conv_second.shape, BF16), dma((6,)),
         vm((640, 640), BF16), vm((8, 16, 256), F32), vm((planes, 1, 128), jnp.int32),
         vm((planes, 16, 256), BF16), vm((planes, 16, 256), BF16),
         vm((16 * crops, 256), F32), vm((16 * crops, 256), BF16),
@@ -567,12 +566,12 @@
             jax.ShapeDtypeStruct((2, channels), F32),
             jax.ShapeDtypeStruct((rows_all // groups, channels), F32),
         ],
-        in_specs=[hbm, hbm, hbm, hbm, hbm, hbm, hbm],
+        in_specs=[hbm, vmem, hbm, hbm, hbm, hbm, hbm],
         out_specs=[vmem] * 3,
         scratch_shapes=scratch,
         compiler_params=pltpu.CompilerParams(
             collective_id=0, has_side_effects=True, vmem_limit_bytes=63 * 2**20),
-    )(audio, counts, cotangent, conv_first, norm_gain, norm_bias, conv_second)
+    )(audio, jnp.broadcast_to(counts, (1, 128)), cotangent, conv_first, norm_gain, norm_bias, conv_second)
 
     def place(*refs):
         ins, results, held, sems = refs[0:3], refs[3:6], refs[6:9], refs[9]

time: 65.9 us -> 67 us (1.017)
  the two profiles are of different devices: /device:TPU:1 before, /device:TPU:4 now
where the time goes in v3:
time: 67 us; the launch traced here: 66.9 us
  Pallas kernels  65.1 us (97%)
  between operations  1.28 us (2%)
    pallas_call x1, Pallas kernels, on_device(): pl.pallas_call(functools.partial(kernel, planes, depth, scale), out_shape...  63.5 us
    pallas_call x1, Pallas kernels, on_device(): pl.pallas_call(place, out_shape=[jax.ShapeDtypeStruct(out.shape, out.dtyp...  1.61 us

profile of v3, /device:TPU:4, one launch (start us, length us, event | category | flops | bytes accessed | tf_op | source)
XLA Modules:
  0.0 66.9 jit_solution(14150011970870427202)
XLA Ops:
  1.3 0.5 broadcast_in_dim.8.counts_ref
  1.8 63.5 %shard_map.94 = (f32[10,512]{1,0:T(8,128)}, f32[2,512]{1,0:T(2,128)}, f32[48,512]{1,0:T(8,128)}) custom-call(bf16[1,8,2570]{2,1,0:T(8,128)(2,1)} %audio_hbm.1, s32[1,128]{1,0:T(1,128)} %broadcast_in_dim.8.counts_ref, bf16[1,4,256,512]{3,2,1,0:T(8,128)(2,1)} %cot_hbm.1, bf16[10,512]{1,0:T(8,128)(2,1)} %w1_hbm.1, f32[512]{0:T(512)} %gain_hbm.1, f32[512]{0:T(512)} %bias_hbm.1, ...), custom_call_target="tpu_custom_call" | custom-call | tf_op jit(solution)/shard_map/pallas_call | solution.py:562
  65.2 1.6 %shard_map.95 = (f32[10,512]{1,0:T(8,128)}, f32[2,512]{1,0:T(2,128)}, f32[48,512]{1,0:T(8,128)}) custom-call(f32[10,512]{1,0:T(8,128)} %get-tuple-element.6.refs_0_, f32[2,512]{1,0:T(2,128)} %get-tuple-element.7.refs_1_, f32[48,512]{1,0:T(8,128)} %get-tuple-element.8.refs_2_), custom_call_target="tpu_custom_call" | custom-call | tf_op jit(solution)/shard_map/pallas_call | solution.py:588

commit v4 on v3

--- a/solution.py
+++ b/solution.py
@@ -62,6 +62,18 @@
     z = dy // 2
     px = lax.rem(me, SIDE)
     py = me // SIDE
+    xs = [px] + [lax.rem(px + k, SIDE) for k in range(1, SIDE)]
+    ys = [py * SIDE] + [lax.rem(py + k, SIDE) * SIDE for k in range(1, SIDE)]
+    peers = [ys[k // SIDE] + xs[k % SIDE] for k in range(planes)]
+    column = [2 * lax.rem(z + k, depth) + core for k in range(depth)]
+    other = 2 * z + 1 - core
+    pair = (me, other)
+    few = planes - 1
+
+    def hops(k):
+        return min(k % SIDE, SIDE - k % SIDE) + min(k // SIDE, SIDE - k // SIDE)
+
+    far_first = sorted(range(1, planes), key=lambda k: -hops(k))
     zhalf = depth // 2
     frames = cot_hbm.shape[2]
     channels = w2_hbm.shape[1]
@@ -92,26 +104,19 @@
 
     barrier = pltpu.get_barrier_semaphore()
 
-    @pl.loop(0, planes)
-    def _(p):
-        @pl.when(p != me)
-        def _():
-            pl.semaphore_signal(barrier, inc=1, device_id=(p, dy), device_id_type=MESH)
-
-        pl.semaphore_signal(barrier, inc=1, device_id=(p, 2 * z + 1 - core), device_id_type=MESH)
-
-    @pl.loop(0, depth)
-    def _(k):
-        @pl.when(k != z)
-        def _():
-            pl.semaphore_signal(barrier, inc=1, device_id=(me, 2 * k + core), device_id_type=MESH)
+    for k in range(planes):
+        if k:
+            pl.semaphore_signal(barrier, inc=1, device_id=(peers[k], dy), device_id_type=MESH)
+        pl.semaphore_signal(barrier, inc=1, device_id=(peers[k], other), device_id_type=MESH)
+    for k in range(1, depth):
+        pl.semaphore_signal(barrier, inc=1, device_id=(me, column[k]), device_id_type=MESH)
 
     lane = cols_of((1, 640))
     sample = 10 * (lane % 64) + 2 * (lane // 128) + (lane % 128) // 64
     for i in range(5):
         block = rows_of((128, 640)) + 128 * i
         perm[pl.ds(128 * i, 128), :] = jnp.where(block == sample, 1.0, 0.0).astype(BF16)
-    cnt_all[me] = counts_ref[...]
+    cnt_all[me] = jnp.broadcast_to(counts_ref[...], (1, 128))
 
     loads[0].wait()
     blocks = jnp.concatenate(
@@ -153,15 +158,10 @@
 
     pl.semaphore_wait(barrier, 2 * planes - 1 + depth - 1)
 
-    @pl.loop(1, planes)
-    def _(k):
-        to = lax.rem(me + k, planes)
-        send(cnt_all.at[me], cnt_all.at[me], cnt_ss.at[k], cnt_rs.at[k], (to, dy)).start()
-
-    @pl.loop(1, planes)
-    def _(k):
-        frm = lax.rem(me - k + planes, planes)
-        send(cnt_all.at[me], cnt_all.at[frm], cnt_ss.at[k], cnt_rs.at[k], (frm, dy)).wait()
+    for k in range(1, planes):
+        send(cnt_all.at[me], cnt_all.at[me], cnt_ss.at[0], cnt_rs.at[0], (peers[k], dy)).start()
+    others = cnt_all.at[pl.ds(0, few)]
+    send(others, others, cnt_ss.at[0], cnt_rs.at[0], pair).wait()
 
     count_rows = cnt_all[...].reshape(planes, 128)
     who = rows_of((planes, 128))
@@ -174,10 +174,9 @@
     routed = dot(jnp.where(pick, 1.0, 0.0).astype(BF16), slot_rows).astype(BF16)
     crop_send[...] = routed.reshape(planes, 16, 256)
 
-    @pl.loop(1, planes)
-    def _(k):
-        to = lax.rem(me + k, planes)
-        send(crop_send.at[to], crop_recv.at[me], crop_ss.at[k], crop_rs.at[k], (to, dy)).start()
+    for k in range(1, planes):
+        send(crop_send.at[peers[k]], crop_recv.at[me], crop_ss.at[0], crop_rs.at[0],
+             (peers[k], dy)).start()
 
     crop_recv[me] = crop_send[me]
     wide = jnp.concatenate([count_rows, count_rows], axis=1)
@@ -190,10 +189,8 @@
     pick = (rr % 16 == cc % 16) & (start_col <= order) & (order < start_col + count_col)
     pick = jnp.where(pick, 1.0, 0.0).astype(BF16)
 
-    @pl.loop(1, planes)
-    def _(k):
-        frm = lax.rem(me - k + planes, planes)
-        send(crop_send.at[frm], crop_recv.at[frm], crop_ss.at[k], crop_rs.at[k], (frm, dy)).wait()
+    send(crop_send.at[pl.ds(0, few)], crop_recv.at[pl.ds(0, few)], crop_ss.at[0], crop_rs.at[0],
+         pair).wait()
 
     mine = dot(pick, crop_recv[...].reshape(16 * planes, 256))
     xf[...] = mine
@@ -270,17 +267,12 @@
             grad = (scale * cot[0, r, :, cols].astype(F32)) * slope
             grows[pl.ds(base, frames), cols] = grad.astype(BF16)
 
-    pair = (me, 2 * z + 1 - core)
     for h in range(2):
         theirs = dot(hid[1 - core, :, h * hrows : (h + 1) * hrows], grows[...], TN)
         pair_send[h] = theirs.astype(BF16)
         send(pair_send.at[h], pair_recv.at[h], pair_ss.at[h], pair_rs.at[h], pair).start()
         if h == 0:
             half_sum[0] = dot(hid[core, :, 0:hrows], grows[...], TN)
-
-    def p_copy(h, k, slot, slot_at, where):
-        return send(p_send.at[h, slot], p_recv.at[h, slot_at], plane_ss.at[h, k], plane_rs.at[h, k],
-                    (where, dy))
 
     for h in range(2):
         if h == 1:
@@ -294,10 +286,10 @@
                 [half_sum[h, i * rz + first : i * rz + first + rx, lanes] for i in range(hz)], axis=0
             ).astype(BF16)
 
-        @pl.loop(1, planes)
-        def _(k):
-            to = lax.rem(me + k, planes)
-            p_copy(h, k, to, me, to).start()
+        p_recv[h, me] = jnp.zeros((hz * rx, 128), BF16)
+        for k in far_first:
+            send(p_send.at[h, peers[k]], p_recv.at[h, me], plane_ss.at[h, 0], plane_rs.at[h, 0],
+                 (peers[k], dy)).start()
 
     acc_e[...] = jnp.zeros_like(acc_e)
     acc_o[...] = jnp.zeros_like(acc_o)
@@ -345,123 +337,99 @@
     unit = me // 2
     holder = (lax.rem(me, 2) == 0) & (core == lax.rem(unit, 2))
 
-    @pl.loop(0, units)
-    def _(u):
-        to_core = lax.rem(u, 2)
-
-        @pl.when((me == 2 * u) & (core == to_core))
-        def _():
+    for u in range(units):
+        mine_u = (me == 2 * u) & (core == u % 2)
+
+        @pl.when(mine_u)
+        def _(u=u):
             s_recv[lane_of] = s_send[u]
 
-        @pl.when((me != 2 * u) | (core != to_core))
-        def _():
-            send(s_send.at[u], s_recv.at[lane_of], s1_ss.at[u], s1_rs.at[lane_of],
-                 (2 * u, 2 * z + to_core)).start()
-
-    def u_copy(k, slot_at):
-        return send(u_val, u_recv.at[slot_at], s2_ss.at[k], s2_rs.at[slot_at], (me, 2 * k + core))
-
-    @pl.when(holder)
-    def _():
-        @pl.loop(0, 2 * planes)
-        def _(i):
-            @pl.when(i != lane_of)
-            def _():
-                send(s_send.at[0], s_recv.at[i], s1_ss.at[0], s1_rs.at[i],
-                     (i // 2, 2 * z + lax.rem(i, 2))).wait_recv()
-
-        u_val[...] = jnp.sum(s_recv[...], axis=0)
-
-        @pl.loop(0, depth)
-        def _(k):
-            @pl.when(k != z)
-            def _():
-                u_copy(k, z).start()
+        @pl.when(jnp.logical_not(mine_u))
+        def _(u=u):
+            send(s_send.at[u], s_recv.at[lane_of], s1_ss.at[0], s1_rs.at[0],
+                 (2 * u, 2 * z + u % 2)).start()
 
     mine_rows = pl.multiple_of(px * rx, 8)
     mine_lanes = pl.ds(pl.multiple_of(128 * py, 128), 128)
     pad = z_send.shape[1] - rx
 
-    def z_copy(i, slot_at):
-        return send(z_send.at[i], z_recv.at[slot_at], z_ss.at[i], z_rs.at[slot_at],
-                    (me, 2 * (core * zhalf + i) + core))
+    z_recv[z] = jnp.zeros(z_recv.shape[1:], BF16)
 
     for h in range(2):
         own = jnp.concatenate(
             [half_sum[h, pl.ds(i * rz + mine_rows, rx), mine_lanes] for i in range(hz)], axis=0)
 
-        def add(k, total):
-            frm = lax.rem(me - k + planes, planes)
-            p_copy(h, k, frm, frm, frm).wait()
-            return total + p_recv[h, frm].astype(F32)
-
-        own = lax.fori_loop(1, planes, add, own).reshape(hz, rx, 128)
+        send(p_send.at[h, pl.ds(0, few)], p_recv.at[h, pl.ds(0, few)], plane_ss.at[h, 0],
+             plane_rs.at[h, 0], pair).wait()
+        for p in range(planes):
+            own = own + p_recv[h, p].astype(F32)
+        own = own.reshape(hz, rx, 128)
         part[h * hz : h * hz + hz] = own
         padding = [jnp.zeros((hz, pad, 128), F32)] if pad else []
         z_send[h * hz : h * hz + hz] = jnp.concatenate([own] + padding, axis=1).astype(BF16)
 
-        @pl.loop(h * hz, h * hz + hz)
-        def _(i):
+        for i in range(h * hz, h * hz + hz):
             @pl.when(core * zhalf + i != z)
-            def _():
-                z_copy(i, z).start()
-
-    def v_copy(i, slot_at):
-        return send(v_val, v_recv.at[slot_at], s3_ss.at[i], s3_rs.at[slot_at],
-                    (i // 2, 2 * z + lax.rem(i, 2)))
+            def _(i=i):
+                send(z_send.at[i], z_recv.at[z], z_ss.at[0], z_rs.at[0],
+                     (me, 2 * (core * zhalf + i) + core)).start()
 
     @pl.when(holder)
     def _():
-        v_val[...] = u_val[...]
-
-        @pl.loop(0, depth)
-        def _(k):
-            @pl.when(k != z)
-            def _():
-                u_copy(k, k).wait_recv()
-                v_val[...] += u_recv[k]
-
-        v_recv[unit] = v_val[...]
-
-        @pl.loop(0, 2 * planes)
-        def _(i):
-            @pl.when(i != lane_of)
-            def _():
-                v_copy(i, unit).start()
+        rest = s_recv.at[pl.ds(0, 2 * planes - 1)]
+        send(rest, rest, s1_ss.at[0], s1_rs.at[0], pair).wait_recv()
+        total = jnp.sum(s_recv[...], axis=0)
+        u_val[...] = total
+        u_recv[z] = total
+        for k in range(1, depth):
+            send(u_val, u_recv.at[z], s2_ss.at[0], s2_rs.at[0], (me, column[k])).start()
 
     active = z // zhalf == core
     to_core = px // 2
     mine_at = lax.rem(px, 2) * SIDE + py
 
-    def d_copy(p, slot_at):
-        return send(full, gathered.at[slot_at], d_ss.at[p], d_rs.at[slot_at], (p, 2 * z + to_core))
+    d_to = 2 * z + to_core
 
     @pl.when(active)
     def _():
-        full[...] = part[lax.rem(z, zhalf)]
-
-        @pl.loop(0, depth)
-        def _(k):
-            @pl.when(k != z)
-            def _():
-                send(z_send.at[0], z_recv.at[k], z_ss.at[0], z_rs.at[k],
-                     (me, 2 * k + core)).wait_recv()
-                full[...] += z_recv[k].astype(F32)[0:rx]
+        rest = z_recv.at[pl.ds(0, depth - 1)]
+        send(rest, rest, z_ss.at[0], z_rs.at[0], pair).wait_recv()
+        total = part[lax.rem(z, zhalf)]
+        for k in range(depth):
+            total = total + z_recv[k].astype(F32)[0:rx]
+        full[...] = total
+        for k in range(1, planes):
+            send(full, gathered.at[mine_at], d_ss.at[0], d_rs.at[0], (peers[k], d_to)).start()
 
         @pl.when(to_core == core)
         def _():
             gathered[mine_at] = full[...]
 
-        @pl.loop(0, planes)
-        def _(p):
-            @pl.when((p != me) | (to_core != core))
-            def _():
-                d_copy(p, mine_at).start()
-
-    for u in range(units):
-        @pl.when((me != 2 * u) | (core != u % 2))
-        def _(u=u):
-            v_copy(0, u).wait_recv()
+        @pl.when(to_core != core)
+        def _():
+            send(full, gathered.at[mine_at], d_ss.at[0], d_rs.at[0], pair).start()
+
+    @pl.when(holder)
+    def _():
+        rest = u_recv.at[pl.ds(0, depth - 1)]
+        send(rest, rest, s2_ss.at[0], s2_rs.at[0], pair).wait()
+        total = jnp.sum(u_recv[...], axis=0)
+        v_val[...] = total
+        v_recv[unit] = total
+        for k in range(planes):
+            if k:
+                send(v_val, v_recv.at[unit], s3_ss.at[0], s3_rs.at[0], (peers[k], dy)).start()
+            send(v_val, v_recv.at[unit], s3_ss.at[0], s3_rs.at[0], (peers[k], other)).start()
+        rest = v_recv.at[pl.ds(0, units - 1)]
+        send(rest, rest, s3_ss.at[0], s3_rs.at[0], pair).wait_recv()
+        sent = s_send.at[pl.ds(0, units - 1)]
+        send(sent, sent, s1_ss.at[0], s1_rs.at[0], pair).wait_send()
+
+    @pl.when(jnp.logical_not(holder))
+    def _():
+        send(v_recv, v_recv, s3_ss.at[0], s3_rs.at[0], pair).wait_recv()
+        send(s_send, s_send, s1_ss.at[0], s1_rs.at[0], pair).wait_send()
+
     for u in range(units):
         cols = slice(128 * (u % 4), 128 * (u % 4) + 128)
         if u < 4:
@@ -470,51 +438,44 @@
             first_out[8:10, cols] = v_recv[u, 0:2]
             norm_out[:, cols] = v_recv[u, 2:4]
 
-    owner = z // zhalf
+    lands_here = active & (to_core == core)
+
+    @pl.when(lands_here)
+    def _():
+        rest = gathered.at[pl.ds(0, 2 * SIDE - 1)]
+        send(rest, rest, d_ss.at[0], d_rs.at[0], pair).wait_recv()
+
+    @pl.when(jnp.logical_not(lands_here))
+    def _():
+        rest = gathered.at[pl.ds(0, 2 * SIDE)]
+        send(rest, rest, d_ss.at[0], d_rs.at[0], pair).wait_recv()
+
     for i in range(2):
         for y in range(SIDE):
-            sender = y * SIDE + 2 * core + i
-
-            @pl.when((sender != me) | (owner != core))
-            def _(i=i, y=y):
-                send(full, gathered.at[i * SIDE + y], d_ss.at[0], d_rs.at[i * SIDE + y],
-                     (me, dy + 1 - 2 * core)).wait_recv()
             second_out[rx * i : rx * i + rx, 128 * y : 128 * y + 128] = gathered[i * SIDE + y]
 
-    @pl.loop(0, units)
-    def _(u):
-        @pl.when((me != 2 * u) | (core != lax.rem(u, 2)))
+    @pl.when(holder)
+    def _():
+        sent = s_recv.at[pl.ds(0, 2 * planes - 1)]
+        send(sent, sent, s3_ss.at[0], s3_rs.at[0], pair).wait_send()
+
+    @pl.when(active)
+    def _():
+        sent = z_send.at[pl.ds(0, zhalf - 1)]
+        send(sent, sent, z_ss.at[0], z_rs.at[0], pair).wait_send()
+
+        @pl.when(to_core == core)
         def _():
-            send(s_send.at[u], s_recv.at[lane_of], s1_ss.at[u], s1_rs.at[lane_of],
-                 (2 * u, 2 * z + lax.rem(u, 2))).wait_send()
-
-    @pl.when(holder)
-    def _():
-        @pl.loop(0, depth)
-        def _(k):
-            @pl.when(k != z)
-            def _():
-                u_copy(k, z).wait_send()
-
-        @pl.loop(0, 2 * planes)
-        def _(i):
-            @pl.when(i != lane_of)
-            def _():
-                v_copy(i, unit).wait_send()
-
-    @pl.loop(0, zhalf)
-    def _(i):
-        @pl.when(core * zhalf + i != z)
+            sent = gathered.at[pl.ds(0, planes - 1)]
+            send(sent, sent, d_ss.at[0], d_rs.at[0], pair).wait_send()
+
+        @pl.when(to_core != core)
         def _():
-            z_copy(i, z).wait_send()
-
-    @pl.when(active)
-    def _():
-        @pl.loop(0, planes)
-        def _(p):
-            @pl.when((p != me) | (to_core != core))
-            def _():
-                d_copy(p, mine_at).wait_send()
+            send(gathered, gathered, d_ss.at[0], d_rs.at[0], pair).wait_send()
+
+    @pl.when(jnp.logical_not(active))
+    def _():
+        send(z_send, z_send, z_ss.at[0], z_rs.at[0], pair).wait_send()
 
 
 def on_device(audio, counts, cotangent, conv_first, norm_gain, norm_bias, conv_second):
@@ -549,7 +510,7 @@
         vm((2, hrows, channels), BF16),
         vm((2, planes, hz * rx, 128), BF16), vm((2, planes, hz * rx, 128), BF16),
         vm((zhalf, rx, 128), F32), vm((zhalf, rpad, 128), BF16), vm((depth, rpad, 128), BF16),
-        vm((rx, 128), F32), vm((8, rx, 128), F32),
+        vm((rx, 128), F32), vm((planes, rx, 128), F32),
         vm((16, channels), F32), vm((16, channels), F32), vm((8, channels), F32),
         vm((16, channels), F32), vm((8, 8, 128), F32), vm((2 * planes, 8, 128), F32),
         vm((8, 128), F32), vm((depth, 8, 128), F32), vm((8, 128), F32), vm((8, 8, 128), F32),
@@ -571,7 +532,7 @@
         scratch_shapes=scratch,
         compiler_params=pltpu.CompilerParams(
             collective_id=0, has_side_effects=True, vmem_limit_bytes=63 * 2**20),
-    )(audio, jnp.broadcast_to(counts, (1, 128)), cotangent, conv_first, norm_gain, norm_bias, conv_second)
+    )(audio, counts, cotangent, conv_first, norm_gain, norm_bias, conv_second)
 
     def place(*refs):
         ins, results, held, sems = refs[0:3], refs[3:6], refs[6:9], refs[9]

time: 67 us -> 64.7 us (0.966)
  the two profiles are of different devices: /device:TPU:4 before, /device:TPU:1 now
where the time goes in v4:
time: 64.7 us; the launch traced here: 64.6 us
  Pallas kernels  63.3 us (98%)
  between operations  1.29 us (2%)
    pallas_call x1, Pallas kernels, on_device(): pl.pallas_call(functools.partial(kernel, planes, depth, scale), out_shape...  61.7 us
    pallas_call x1, Pallas kernels, on_device(): pl.pallas_call(place, out_shape=[jax.ShapeDtypeStruct(out.shape, out.dtyp...  1.61 us

profile of v4, /device:TPU:1, one launch (start us, length us, event | category | flops | bytes accessed | tf_op | source)
XLA Modules:
  0.0 64.6 jit_solution(10423236085287256570)
XLA Ops:
  1.3 61.7 %shard_map.94 = (f32[10,512]{1,0:T(8,128)}, f32[2,512]{1,0:T(2,128)}, f32[48,512]{1,0:T(8,128)}) custom-call(bf16[1,8,2570]{2,1,0:T(8,128)(2,1)} %audio_hbm.1, s32[1,1]{1,0:T(1,128)S(6)} %copy.10.counts_ref, bf16[1,4,256,512]{3,2,1,0:T(8,128)(2,1)} %cot_hbm.1, bf16[10,512]{1,0:T(8,128)(2,1)} %w1_hbm.1, f32[512]{0:T(512)} %gain_hbm.1, f32[512]{0:T(512)} %bias_hbm.1, ...), custom_call_target="tpu_custom_call" | custom-call | tf_op jit(solution)/shard_map/pallas_call | solution.py:523
  62.9 1.6 %shard_map.95 = (f32[10,512]{1,0:T(8,128)}, f32[2,512]{1,0:T(2,128)}, f32[48,512]{1,0:T(8,128)}) custom-call(f32[10,512]{1,0:T(8,128)} %get-tuple-element.6.refs_0_, f32[2,512]{1,0:T(2,128)} %get-tuple-element.7.refs_1_, f32[48,512]{1,0:T(8,128)} %get-tuple-element.8.refs_2_), custom_call_target="tpu_custom_call" | custom-call | tf_op jit(solution)/shard_map/pallas_call | solution.py:549

commit v5 on v4

--- a/solution.py
+++ b/solution.py
@@ -55,6 +55,7 @@
     acc_e, acc_o, acc_t, small, s_send, s_recv, u_val, u_recv, v_val, v_recv,
     cnt_ss, cnt_rs, crop_ss, crop_rs, pair_ss, pair_rs, plane_ss, plane_rs,
     z_ss, z_rs, d_ss, d_rs, s1_ss, s1_rs, s2_ss, s2_rs, s3_ss, s3_rs,
+    from_below, from_above,
 ):
     me = lax.axis_index("dx")
     dy = lax.axis_index("dy")
@@ -108,8 +109,19 @@
         if k:
             pl.semaphore_signal(barrier, inc=1, device_id=(peers[k], dy), device_id_type=MESH)
         pl.semaphore_signal(barrier, inc=1, device_id=(peers[k], other), device_id_type=MESH)
-    for k in range(1, depth):
+    for k in (1, depth - 1):
         pl.semaphore_signal(barrier, inc=1, device_id=(me, column[k]), device_id_type=MESH)
+    rounds = depth // 2 - 1
+
+    def tell(j):
+        if j <= rounds:
+            pl.semaphore_signal(from_below.at[j - 1], inc=1, device_id=(me, column[1]), device_id_type=MESH)
+            pl.semaphore_signal(from_above.at[j - 1], inc=1, device_id=(me, column[depth - 1]), device_id_type=MESH)
+
+    def hear(j):
+        if j <= rounds:
+            pl.semaphore_wait(from_below.at[j - 1], 1)
+            pl.semaphore_wait(from_above.at[j - 1], 1)
 
     lane = cols_of((1, 640))
     sample = 10 * (lane % 64) + 2 * (lane // 128) + (lane % 128) // 64
@@ -156,13 +168,16 @@
     wpad[...] = jnp.zeros_like(wpad)
     wpad[0:10, :] = w1v
 
-    pl.semaphore_wait(barrier, 2 * planes - 1 + depth - 1)
+    pl.semaphore_wait(barrier, 2 * planes - 1 + 2)
+    tell(1)
 
     for k in range(1, planes):
         send(cnt_all.at[me], cnt_all.at[me], cnt_ss.at[0], cnt_rs.at[0], (peers[k], dy)).start()
     others = cnt_all.at[pl.ds(0, few)]
     send(others, others, cnt_ss.at[0], cnt_rs.at[0], pair).wait()
 
+    hear(1)
+    tell(2)
     count_rows = cnt_all[...].reshape(planes, 128)
     who = rows_of((planes, 128))
     start_me = jnp.sum(jnp.where(who < me, count_rows, 0), axis=0, keepdims=True)
@@ -192,6 +207,8 @@
     send(crop_send.at[pl.ds(0, few)], crop_recv.at[pl.ds(0, few)], crop_ss.at[0], crop_rs.at[0],
          pair).wait()
 
+    hear(2)
+    tell(3)
     mine = dot(pick, crop_recv[...].reshape(16 * planes, 256))
     xf[...] = mine
     xp_all = jnp.where(rows_of((16 * crops, 256)) % 16 == 10, 1.0, mine)
@@ -233,6 +250,8 @@
                 waug[r, 64 * i + 16 * r : 64 * i + 16 * r + 16,
                      side * channels : (side + 1) * channels] = piece
 
+    hear(3)
+    tell(4)
     loads[4].wait()
     loads[5].wait()
     quarter = channels // 2
@@ -266,6 +285,8 @@
             slope = gelu_parts(pre)[1]
             grad = (scale * cot[0, r, :, cols].astype(F32)) * slope
             grows[pl.ds(base, frames), cols] = grad.astype(BF16)
+        hear(r + 4)
+        tell(r + 5)
 
     for h in range(2):
         theirs = dot(hid[1 - core, :, h * hrows : (h + 1) * hrows], grows[...], TN)
@@ -517,6 +538,7 @@
         dma((planes,)), dma((planes,)), dma((planes,)), dma((planes,)), dma((2,)), dma((2,)),
         dma((2, planes)), dma((2, planes)), dma((zhalf,)), dma((depth,)), dma((planes,)), dma((8,)),
         dma((8,)), dma((2 * planes,)), dma((depth,)), dma((depth,)), dma((2 * planes,)), dma((8,)),
+        pltpu.SemaphoreType.REGULAR((8,)), pltpu.SemaphoreType.REGULAR((8,)),
     ]
     hbm = pl.BlockSpec(memory_space=pltpu.HBM)
     vmem = pl.BlockSpec(memory_space=pltpu.VMEM)

time: 64.7 us -> 65.9 us (1.019)
  Pallas kernels: 63.3 us -> 64.5 us
    pallas_call x1, Pallas kernels: 61.7 us -> 62.8 us  [on_device(): pl.pallas_call(functools.partial(kernel, planes, depth, scale), out_shape...]
where the time goes in v5:
time: 65.9 us; the launch traced here: 65.7 us
  Pallas kernels  64.5 us (98%)
  between operations  1.29 us (2%)
    pallas_call x1, Pallas kernels, on_device(): pl.pallas_call(functools.partial(kernel, planes, depth, scale), out_shape...  62.8 us
    pallas_call x1, Pallas kernels, on_device(): pl.pallas_call(place, out_shape=[jax.ShapeDtypeStruct(out.shape, out.dtyp...  1.61 us

profile of v5, /device:TPU:1, one launch (start us, length us, event | category | flops | bytes accessed | tf_op | source)
XLA Modules:
  0.0 65.7 jit_solution(9447627820191455483)
XLA Ops:
  1.3 62.8 %shard_map.94 = (f32[10,512]{1,0:T(8,128)}, f32[2,512]{1,0:T(2,128)}, f32[48,512]{1,0:T(8,128)}) custom-call(bf16[1,8,2570]{2,1,0:T(8,128)(2,1)} %audio_hbm.1, s32[1,1]{1,0:T(1,128)S(6)} %copy.10.counts_ref, bf16[1,4,256,512]{3,2,1,0:T(8,128)(2,1)} %cot_hbm.1, bf16[10,512]{1,0:T(8,128)(2,1)} %w1_hbm.1, f32[512]{0:T(512)} %gain_hbm.1, f32[512]{0:T(512)} %bias_hbm.1, ...), custom_call_target="tpu_custom_call" | custom-call | tf_op jit(solution)/shard_map/pallas_call | solution.py:545
  64.1 1.6 %shard_map.95 = (f32[10,512]{1,0:T(8,128)}, f32[2,512]{1,0:T(2,128)}, f32[48,512]{1,0:T(8,128)}) custom-call(f32[10,512]{1,0:T(8,128)} %get-tuple-element.6.refs_0_, f32[2,512]{1,0:T(2,128)} %get-tuple-element.7.refs_1_, f32[48,512]{1,0:T(8,128)} %get-tuple-element.8.refs_2_), custom_call_target="tpu_custom_call" | custom-call | tf_op jit(solution)/shard_map/pallas_call | solution.py:571
